TPU v7x, 32 devices: a whole 2x2x4 slice. The times are simulated.
32 devices in a mesh: blk: 8 (over z, y), head: 4 (over x, core).
Axes of the slice: x: 2, y: 2, z: 4, core: 2. Of those that a mesh axis runs over, the one named last changes fastest.
Arguments:
- tokens: bfloat16 [2, 2048, 2048], P(None, ('blk', 'head')), may hold values from -6 to 6
- cotangent: float32 [2, 2048, 2048], P(None, ('blk', 'head')), may hold values from -6 to 6
- lengths: int32 [2], replicated, may hold values from 1024 to 2048, as said below
- routes: int32 [2, 2048, 8], P(None, ('blk', 'head')), may hold values from 0 to 63, all different within a row; in each aligned block of 64 rows (0 to 63, 64 to 127, ..., all dimensions but the last counted through in order) at most 12 rows name the same one
- attn_gain: bfloat16 [2048], P(('blk', 'head')), may hold values from 0.5 to 1.5
- w_query: bfloat16 [2048, 2048], P(('blk', 'head')), may hold values from -0.1875 to 0.1875
- w_key: bfloat16 [2048, 2048], P(('blk', 'head')), may hold values from -0.1875 to 0.1875
- w_value: bfloat16 [2048, 2048], P(('blk', 'head')), may hold values from -0.125 to 0.125
- w_out: bfloat16 [2048, 2048], P(('blk', 'head')), may hold values from -1.5 to 1.5
- ffn_gain: bfloat16 [2048], P(('blk', 'head')), may hold values from 0.5 to 1.5
- w_router: bfloat16 [2048, 64], P(('blk', 'head')), may hold values from -0.0625 to 0.0625
- w_gate: bfloat16 [64, 2048, 1024], P('blk', 'head'), may hold values from -0.125 to 0.125
- w_up: bfloat16 [64, 2048, 1024], P('blk', 'head'), may hold values from -0.125 to 0.125
- w_down: bfloat16 [64, 1024, 2048], P('blk', 'head'), may hold values from -6 to 6
Outputs:
- output: bfloat16 [2, 2048, 2048], P(None, ('blk', 'head'))
- grad_tokens: float32 [2, 2048, 2048], P(None, ('blk', 'head'))
- grad_attn_gain: float32 [2048], P(('blk', 'head'))
- grad_query: float32 [2048, 2048], P(('blk', 'head'))
- grad_key: float32 [2048, 2048], P(('blk', 'head'))
- grad_value: float32 [2048, 2048], P(('blk', 'head'))
- grad_out: float32 [2048, 2048], P(('blk', 'head'))
- grad_ffn_gain: float32 [2048], P(('blk', 'head'))
- grad_router: float32 [2048, 64], P(('blk', 'head'))
- grad_gate: float32 [64, 2048, 1024], P('blk', 'head')
- grad_up: float32 [64, 2048, 1024], P('blk', 'head')
- grad_down: float32 [64, 1024, 2048], P('blk', 'head')
Inputs may be any that keep to these rules, and one draw needn't show every extreme that they name: `lengths`: one sequence, drawn from the seed, has length 2048. `routes`: each token names 8 different experts; in each aligned block of 64 rows (tokens in order of sequence, then position) no expert is named by more than 12 rows, and one expert by exactly 12.
All inputs are finite; a program needn't handle non-finite values.
Results may differ from a plain program's by a relative error of at most 0.018.
The roundings to bfloat16 on the way count: a program that leaves them out, or rounds other values in their place, can miss the bound.
Values may be sent and summed in bfloat16 or wider, within the bound.
A program may use at most 576 MiB of HBM per device.

v0:
```python
import functools

import jax
import jax.numpy as jnp
from jax import lax
from jax.experimental import pallas as pl
from jax.experimental.pallas import tpu as pltpu
from jax.sharding import Mesh
from jax.sharding import PartitionSpec as P

HEADS = 16
HD = 128
E = 64
TOP = 8
MOST = 12


epsilon = 1e-06
big_negative = -1e30


def key_validity(first_row, count_keys, lengths):
    positions = first_row + jnp.arange(count_keys, dtype=jnp.int32)
    return (positions[None, :] < lengths[:, None])[:, None, None, :]


def norm_backward(grad_normed, normed, inverse):
    return inverse * (grad_normed - normed * jnp.mean(grad_normed * normed, axis=-1, keepdims=True))


def take_sequence(tree, index):
    return jax.tree.map(lambda leaf: leaf[index : index + 1], tree)


def join_sequences(trees):
    return jax.tree.map(lambda *leaves: jnp.concatenate(leaves, axis=0), *trees)


def general_device(
    tokens,
    cotangent,
    lengths,
    routes,
    attn_gain,
    w_query,
    w_key,
    w_value,
    w_out,
    ffn_gain,
    w_router,
    w_gate,
    w_up,
    w_down,
):
    seq_count, sub_rows, width = tokens.shape
    capacity = seq_count * MOST
    score_scale = HD ** (-0.5)
    wq_full, wk_full, wv_full, wo_full, router_full, gain_one, gain_two = (
        lax.all_gather(w_query, ("blk", "head"), axis=0, tiled=True),
        lax.all_gather(w_key, ("blk", "head"), axis=0, tiled=True),
        lax.all_gather(w_value, ("blk", "head"), axis=0, tiled=True),
        lax.all_gather(w_out, ("blk", "head"), axis=0, tiled=True),
        lax.all_gather(w_router, ("blk", "head"), axis=0, tiled=True),
        lax.all_gather(attn_gain, ("blk", "head"), axis=0, tiled=True),
        lax.all_gather(ffn_gain, ("blk", "head"), axis=0, tiled=True),
    )
    gate_full, up_full, down_full = (
        lax.all_gather(w_gate, "head", axis=1, tiled=True),
        lax.all_gather(w_up, "head", axis=1, tiled=True),
        lax.all_gather(w_down, "head", axis=1, tiled=True),
    )
    gain_one_f = gain_one.astype(jnp.float32)
    gain_two_f = gain_two.astype(jnp.float32)
    tokens_f = tokens.astype(jnp.float32)
    inverse_one = lax.rsqrt(jnp.mean(tokens_f * tokens_f, axis=-1, keepdims=True) + epsilon)
    normed_one = tokens_f * inverse_one
    act_one = (normed_one * gain_one_f).astype(jnp.bfloat16)

    def project(weight):
        return (
            jnp.dot(act_one, weight, preferred_element_type=jnp.float32)
            .astype(jnp.bfloat16)
            .reshape(seq_count, sub_rows, HEADS, HD)
        )

    q_heads, k_heads, v_heads = (
        lax.all_to_all(project(wq_full), "head", split_axis=2, concat_axis=1, tiled=True),
        lax.all_to_all(project(wk_full), "head", split_axis=2, concat_axis=1, tiled=True),
        lax.all_to_all(project(wv_full), "head", split_axis=2, concat_axis=1, tiled=True),
    )
    local_rows = q_heads.shape[1]
    local_heads = q_heads.shape[2]
    key_start = lax.axis_index("blk") * local_rows

    def guard_keys(make_step, extras):

        def skipping(state_now, pieces, first_row):
            results = []
            for index in range(seq_count):
                state_one = take_sequence(state_now, index)
                pieces_one = take_sequence(pieces, index)
                step_one = make_step(take_sequence(extras, index), lengths[index : index + 1])
                results.append(
                    lax.cond(
                        first_row < lengths[index],
                        lambda: step_one(state_one, pieces_one, first_row),
                        lambda: state_one,
                    )
                )
            return join_sequences(results)

        return skipping

    def over_keys(block_step, initial):
        return block_step(
            initial,
            (
                lax.all_gather(k_heads, "blk", axis=1, tiled=True),
                lax.all_gather(v_heads, "blk", axis=1, tiled=True),
            ),
            jnp.int32(0),
        )

    def make_forward(extras, lens):
        queries = extras[0]

        def forward_step(state_now, pieces, first_row):
            run_max, run_total, run_sum = state_now
            k_piece, v_piece = pieces
            scores = (
                jnp.einsum("nqhd,nkhd->nqhk", queries, k_piece, preferred_element_type=jnp.float32)
                * score_scale
            )
            valid = key_validity(first_row, k_piece.shape[1], lens)
            new_max = jnp.maximum(run_max, jnp.max(jnp.where(valid, scores, big_negative), axis=-1))
            weights = jnp.where(valid, jnp.exp(scores - new_max[..., None]), 0.0)
            new_total = jnp.sum(weights, axis=-1)
            new_sum = jnp.einsum(
                "nqhk,nkhd->nqhd",
                weights.astype(jnp.bfloat16),
                v_piece,
                preferred_element_type=jnp.float32,
            )
            return (new_max, new_total, new_sum)

        return forward_step

    stats_shape = (seq_count, local_rows, local_heads)
    start_state = (
        jnp.full(stats_shape, big_negative, jnp.float32),
        jnp.zeros(stats_shape, jnp.float32),
        jnp.zeros(q_heads.shape, jnp.float32),
    )
    run_max, run_total, run_sum = over_keys(guard_keys(make_forward, (q_heads,)), start_state)
    attended = (run_sum / run_total[..., None]).astype(jnp.bfloat16)
    log_total = run_max + jnp.log(run_total)
    attended_tok = lax.all_to_all(
        attended, "head", split_axis=1, concat_axis=2, tiled=True
    ).reshape(seq_count, sub_rows, width)
    resid = tokens_f + jnp.dot(attended_tok, wo_full, preferred_element_type=jnp.float32)
    inverse_two = lax.rsqrt(jnp.mean(resid * resid, axis=-1, keepdims=True) + epsilon)
    normed_two = resid * inverse_two
    act_two = (normed_two * gain_two_f).astype(jnp.bfloat16)
    logits = jnp.dot(act_two, router_full, preferred_element_type=jnp.float32)
    probs = jax.nn.softmax(logits, axis=-1)
    expert_ids = jnp.arange(E, dtype=jnp.int32)
    chosen = routes[..., None] == expert_ids
    gates = jnp.sum(jnp.where(chosen, probs[:, :, None, :], 0.0), axis=-1)
    flat_routes = routes.reshape(seq_count, sub_rows * TOP)
    onehot = (flat_routes[..., None] == expert_ids).astype(jnp.int32)
    ranking = jnp.sum(jnp.cumsum(onehot, axis=1) * onehot, axis=-1) - 1
    slot_index = (
        flat_routes * capacity + jnp.arange(seq_count, dtype=jnp.int32)[:, None] * MOST + ranking
    ).reshape(-1)
    assign_count = seq_count * sub_rows * TOP
    source_of = (
        jnp.full((E * capacity,), assign_count, jnp.int32)
        .at[slot_index]
        .set(jnp.arange(assign_count, dtype=jnp.int32))
    )
    padded_rows = jnp.concatenate([act_two.reshape(-1, width), jnp.zeros((1, width), jnp.bfloat16)])
    send_rows = padded_rows[source_of // TOP].reshape(E, capacity, width)

    def to_owners(buffer):
        return lax.all_to_all(buffer, "blk", split_axis=0, concat_axis=1, tiled=True)

    def to_sources(buffer):
        return lax.all_to_all(buffer, "blk", split_axis=1, concat_axis=0, tiled=True)

    expert_in = to_owners(send_rows)
    gate_pre = jnp.einsum("esd,edf->esf", expert_in, gate_full, preferred_element_type=jnp.float32)
    up_pre = jnp.einsum("esd,edf->esf", expert_in, up_full, preferred_element_type=jnp.float32)
    sigmoid = jax.nn.sigmoid(gate_pre)
    swished = gate_pre * sigmoid
    hidden = (swished * up_pre).astype(jnp.bfloat16)
    expert_out = jnp.einsum(
        "esf,efd->esd", hidden, down_full, preferred_element_type=jnp.float32
    ).astype(jnp.bfloat16)
    returned = to_sources(expert_out).reshape(E * capacity, width)
    picked = returned[slot_index].reshape(seq_count, sub_rows, TOP, width).astype(jnp.float32)
    moe_out = jnp.sum(picked * gates[..., None], axis=2)
    output = (resid + moe_out).astype(jnp.bfloat16)
    d_gates = jnp.sum(picked * cotangent[:, :, None, :], axis=-1)
    d_picked = (gates[..., None] * cotangent[:, :, None, :]).astype(jnp.bfloat16).reshape(-1, width)
    d_send = jnp.concatenate([d_picked, jnp.zeros((1, width), jnp.bfloat16)])[source_of].reshape(
        E, capacity, width
    )
    d_expert_out = to_owners(d_send)
    d_hidden = jnp.einsum(
        "esd,efd->esf", d_expert_out, down_full, preferred_element_type=jnp.float32
    )
    grad_down = jnp.einsum("esf,esd->efd", hidden, d_expert_out, preferred_element_type=jnp.float32)
    d_gate_pre = (d_hidden * up_pre * (sigmoid * (1.0 + gate_pre * (1.0 - sigmoid)))).astype(
        jnp.bfloat16
    )
    d_up_pre = (d_hidden * swished).astype(jnp.bfloat16)
    grad_gate = jnp.einsum(
        "esd,esf->edf", expert_in, d_gate_pre, preferred_element_type=jnp.float32
    )
    grad_up = jnp.einsum("esd,esf->edf", expert_in, d_up_pre, preferred_element_type=jnp.float32)
    d_expert_in = (
        jnp.einsum("esf,edf->esd", d_gate_pre, gate_full, preferred_element_type=jnp.float32)
        + jnp.einsum("esf,edf->esd", d_up_pre, up_full, preferred_element_type=jnp.float32)
    ).astype(jnp.bfloat16)
    grad_gate_part, grad_up_part, grad_down_part = (
        lax.psum_scatter(grad_gate, "head", scatter_dimension=1, tiled=True),
        lax.psum_scatter(grad_up, "head", scatter_dimension=1, tiled=True),
        lax.psum_scatter(grad_down, "head", scatter_dimension=1, tiled=True),
    )
    d_returned = to_sources(d_expert_in).reshape(E * capacity, width)
    d_act_routes = jnp.sum(
        d_returned[slot_index].reshape(seq_count, sub_rows, TOP, width).astype(jnp.float32), axis=2
    )
    d_probs = jnp.sum(jnp.where(chosen, d_gates[..., None], 0.0), axis=2)
    d_logits = (probs * (d_probs - jnp.sum(probs * d_probs, axis=-1, keepdims=True))).astype(
        jnp.bfloat16
    )
    grad_router = jnp.einsum("nsd,nse->de", act_two, d_logits, preferred_element_type=jnp.float32)
    d_act_two = d_act_routes + jnp.einsum(
        "nse,de->nsd", d_logits, router_full, preferred_element_type=jnp.float32
    )
    grad_gain_two = jnp.sum(d_act_two * normed_two, axis=(0, 1))
    d_resid = cotangent + norm_backward(d_act_two * gain_two_f, normed_two, inverse_two)
    d_attn = d_resid.astype(jnp.bfloat16)
    grad_wo = jnp.einsum("nsk,nsd->kd", attended_tok, d_attn, preferred_element_type=jnp.float32)
    d_attended = (
        jnp.einsum("nsd,kd->nsk", d_attn, wo_full, preferred_element_type=jnp.float32)
        .astype(jnp.bfloat16)
        .reshape(seq_count, sub_rows, HEADS, HD)
    )
    d_heads = lax.all_to_all(d_attended, "head", split_axis=2, concat_axis=1, tiled=True)
    delta = jnp.sum(d_heads.astype(jnp.float32) * attended.astype(jnp.float32), axis=-1)

    def make_query(extras, lens):
        queries, d_rows, lse_rows, delta_rows = extras

        def query_step(state_now, pieces, first_row):
            k_piece, v_piece = pieces
            scores = (
                jnp.einsum("nqhd,nkhd->nqhk", queries, k_piece, preferred_element_type=jnp.float32)
                * score_scale
            )
            valid = key_validity(first_row, k_piece.shape[1], lens)
            chances = jnp.where(valid, jnp.exp(scores - lse_rows[..., None]), 0.0)
            d_chances = jnp.einsum(
                "nqhd,nkhd->nqhk", d_rows, v_piece, preferred_element_type=jnp.float32
            )
            d_scores = (chances * (d_chances - delta_rows[..., None])).astype(jnp.bfloat16)
            return (
                jnp.einsum("nqhk,nkhd->nqhd", d_scores, k_piece, preferred_element_type=jnp.float32)
                * score_scale
            )

        return query_step

    dq_acc = over_keys(
        guard_keys(make_query, (q_heads, d_heads, log_total, delta)),
        jnp.zeros(q_heads.shape, jnp.float32),
    )

    def key_compute(pieces, keys_here, values_here, lens):
        key_valid = key_validity(key_start, local_rows, lens)
        q_piece = pieces[0].astype(jnp.bfloat16)
        d_piece = pieces[1].astype(jnp.bfloat16)
        lse_piece = pieces[2]
        delta_piece = pieces[3]
        scores = (
            jnp.einsum("nqhd,nkhd->nqhk", q_piece, keys_here, preferred_element_type=jnp.float32)
            * score_scale
        )
        chances = jnp.where(key_valid, jnp.exp(scores - lse_piece[..., None]), 0.0)
        new_dv = jnp.einsum(
            "nqhk,nqhd->nkhd",
            chances.astype(jnp.bfloat16),
            d_piece,
            preferred_element_type=jnp.float32,
        )
        d_chances = jnp.einsum(
            "nqhd,nkhd->nqhk", d_piece, values_here, preferred_element_type=jnp.float32
        )
        d_scores = (chances * (d_chances - delta_piece[..., None])).astype(jnp.bfloat16)
        new_dk = (
            jnp.einsum("nqhk,nqhd->nkhd", d_scores, q_piece, preferred_element_type=jnp.float32)
            * score_scale
        )
        return (new_dk, new_dv)

    zero_grads = jnp.zeros(k_heads.shape, jnp.float32)
    state_now = (zero_grads, zero_grads)
    pieces = (
        lax.all_gather(q_heads.astype(jnp.float32), "blk", axis=1, tiled=True),
        lax.all_gather(d_heads.astype(jnp.float32), "blk", axis=1, tiled=True),
        lax.all_gather(log_total, "blk", axis=1, tiled=True),
        lax.all_gather(delta, "blk", axis=1, tiled=True),
    )
    results = []
    for index in range(seq_count):
        state_one = take_sequence(state_now, index)
        pieces_one = take_sequence(pieces, index)
        keys_one = k_heads[index : index + 1]
        values_one = v_heads[index : index + 1]
        lens_one = lengths[index : index + 1]
        results.append(
            lax.cond(
                key_start < lengths[index],
                lambda: key_compute(pieces_one, keys_one, values_one, lens_one),
                lambda: state_one,
            )
        )
    dk_acc, dv_acc = join_sequences(results)
    dq_tok, dk_tok, dv_tok = (
        lax.all_to_all(
            dq_acc.astype(jnp.bfloat16), "head", split_axis=1, concat_axis=2, tiled=True
        ),
        lax.all_to_all(
            dk_acc.astype(jnp.bfloat16), "head", split_axis=1, concat_axis=2, tiled=True
        ),
        lax.all_to_all(
            dv_acc.astype(jnp.bfloat16), "head", split_axis=1, concat_axis=2, tiled=True
        ),
    )
    dq_flat = dq_tok.reshape(seq_count, sub_rows, width)
    dk_flat = dk_tok.reshape(seq_count, sub_rows, width)
    dv_flat = dv_tok.reshape(seq_count, sub_rows, width)
    grad_wq = jnp.einsum("nsd,nsk->dk", act_one, dq_flat, preferred_element_type=jnp.float32)
    grad_wk = jnp.einsum("nsd,nsk->dk", act_one, dk_flat, preferred_element_type=jnp.float32)
    grad_wv = jnp.einsum("nsd,nsk->dk", act_one, dv_flat, preferred_element_type=jnp.float32)
    d_act_one = jnp.einsum("nsk,dk->nsd", dq_flat, wq_full, preferred_element_type=jnp.float32)
    d_act_one = d_act_one + jnp.einsum(
        "nsk,dk->nsd", dk_flat, wk_full, preferred_element_type=jnp.float32
    )
    d_act_one = d_act_one + jnp.einsum(
        "nsk,dk->nsd", dv_flat, wv_full, preferred_element_type=jnp.float32
    )
    grad_gain_one = jnp.sum(d_act_one * normed_one, axis=(0, 1))
    grad_tokens = d_resid + norm_backward(d_act_one * gain_one_f, normed_one, inverse_one)
    part_wq, part_wk, part_wv, part_wo, part_router, part_gain_one, part_gain_two = (
        lax.psum_scatter(grad_wq, ("blk", "head"), scatter_dimension=0, tiled=True),
        lax.psum_scatter(grad_wk, ("blk", "head"), scatter_dimension=0, tiled=True),
        lax.psum_scatter(grad_wv, ("blk", "head"), scatter_dimension=0, tiled=True),
        lax.psum_scatter(grad_wo, ("blk", "head"), scatter_dimension=0, tiled=True),
        lax.psum_scatter(grad_router, ("blk", "head"), scatter_dimension=0, tiled=True),
        lax.psum_scatter(grad_gain_one, ("blk", "head"), scatter_dimension=0, tiled=True),
        lax.psum_scatter(grad_gain_two, ("blk", "head"), scatter_dimension=0, tiled=True),
    )
    return (
        output,
        grad_tokens,
        part_gain_one,
        part_wq,
        part_wk,
        part_wv,
        part_wo,
        part_gain_two,
        part_router,
        grad_gate_part,
        grad_up_part,
        grad_down_part,
    )


ALL = ("z", "y", "x", "core")
CHIPS = ("z", "y", "x")
HEAD_AXES = ("z", "y", "core")
BF = jnp.bfloat16
F32 = jnp.float32
LOG2E = 1.4426950408889634
GROUP = 256
VMEM_LIMIT = 60 * 1024 * 1024


def swap_x(value):
    return lax.ppermute(value, "x", [(0, 1), (1, 0)])


def swap_core(value):
    return lax.ppermute(value, "core", [(0, 1), (1, 0)])


def swap_head(value, k):
    return lax.ppermute(value, ("x", "core"), [(i, i ^ k) for i in range(4)])


def pick(value, index):
    return lax.dynamic_index_in_dim(value, index, 0, keepdims=False)


def in_order(index, own, other, axis=0):
    return jnp.where(
        index == 0,
        jnp.concatenate([own, other], axis=axis),
        jnp.concatenate([other, own], axis=axis),
    )


def to_everyone(value, axes, count):
    copies = jnp.broadcast_to(value[None], (count,) + value.shape)
    return lax.all_to_all(copies, axes, split_axis=0, concat_axis=0, tiled=True)


def sum_to_owners(value, axes, count):
    pieces = value.reshape((count, value.shape[0] // count) + value.shape[1:])
    pieces = lax.all_to_all(pieces, axes, split_axis=0, concat_axis=0, tiled=True)
    return jnp.sum(pieces.astype(F32), axis=0)


def to_middle(value, x):
    return in_order(x, pick(value, x), swap_x(pick(value, 1 - x)))


def from_middle(value, x):
    halves = value.reshape((2, value.shape[0] // 2) + value.shape[1:])
    own, other = pick(halves, x), swap_x(pick(halves, 1 - x))
    return in_order(x, own[None], other[None])


def nt(a, b):
    return lax.dot_general(a, b, (((1,), (1,)), ((), ())), preferred_element_type=F32)


def nn(a, b):
    return lax.dot_general(a, b, (((1,), (0,)), ((), ())), preferred_element_type=F32)


def tn(a, b):
    return lax.dot_general(a, b, (((0,), (0,)), ((), ())), preferred_element_type=F32)


MESH = pl.DeviceIdType.MESH


def whereabouts():
    return {name: lax.axis_index(name) for name in ALL}


def moved(me, axis, to):
    return tuple(to if name == axis else me[name] for name in ALL)


def plane_index(me):
    return (me["z"] * 2 + me["y"]) * 2 + me["core"]


def plane_device(me, index):
    place = {"z": index // 4, "y": (index // 2) % 2, "x": me["x"], "core": index % 2}
    return tuple(place[name] for name in ALL)


def device_at(index):
    return tuple((index // 8, (index // 4) % 2, (index // 2) % 2, index % 2))


def greet(me, depth, axes, plane=0, every=0):
    barrier = pltpu.get_barrier_semaphore()
    z = me["z"]
    if every:
        place = plane_index(me) // 2 * 4 + me["x"] * 2 + me["core"]

        def hail(i, carry):
            pl.semaphore_signal(barrier, inc=1, device_id=device_at(place ^ i), device_id_type=MESH)
            return carry

        lax.fori_loop(1, every, hail, 0)
        pl.semaphore_wait(barrier, every - 1)
        return
    if plane:
        here = plane_index(me)

        def hello(i, carry):
            pl.semaphore_signal(barrier, inc=1, device_id=plane_device(me, here ^ i), device_id_type=MESH)
            return carry

        lax.fori_loop(1, plane, hello, 0)
        pl.semaphore_wait(barrier, plane - 1)
        return
    for axis in axes:
        pl.semaphore_signal(barrier, inc=1, device_id=moved(me, axis, 1 - me[axis]), device_id_type=MESH)

    @pl.when(z > 0)
    def _():
        pl.semaphore_signal(barrier, inc=1, device_id=moved(me, "z", z - 1), device_id_type=MESH)

    @pl.when(z < depth - 1)
    def _():
        pl.semaphore_signal(barrier, inc=1, device_id=moved(me, "z", z + 1), device_id_type=MESH)

    ends = jnp.where(z > 0, 1, 0) + jnp.where(z < depth - 1, 1, 0)
    pl.semaphore_wait(barrier, len(axes) + ends)


def chip_of(me, flips, oz, turned):
    index = oz
    for axis in ("y", "x"):
        if axis in flips:
            index = index * 2 + (1 - me[axis] if axis in turned else me[axis])
    return index


def along(me, depth, i):
    z = me["z"]
    return jnp.where(z < depth // 2, lax.rem(z + i, depth), lax.rem(z - i + depth, depth))


def spread_kernel(depth, trees, values, mailing, *refs):
    refs = list(refs)
    take = lambda n: [refs.pop(0) for _ in range(n)]
    in_refs = take(values)
    (mail_ref,) = take(1) if mailing else (None,)
    own_refs, other_refs = take(values), take(values)
    (box_ref,) = take(1) if mailing else (None,)
    own_sem, send_sem, recv_sem, core_sem = take(4)
    (mail_sem,) = take(1) if mailing else (None,)
    me = whereabouts()
    z = me["z"]
    flips = trees[0][1]
    plane = mail_ref.shape[0] if mailing else 0
    greet(me, depth, flips + ("core",), plane)
    mine = chip_of(me, flips, z, ())
    locals_ = [
        pltpu.make_async_copy(in_refs[v], own_refs[v].at[mine], own_sem.at[v]) for v in range(values)
    ]
    for local in locals_:
        local.start()
    here = plane_index(me)

    def letter(i, side):
        return pltpu.make_async_remote_copy(
            src_ref=mail_ref.at[here ^ i, side],
            dst_ref=box_ref.at[here // 2, side, me["core"]],
            send_sem=mail_sem.at[0, i, side],
            recv_sem=mail_sem.at[1, i, side],
            device_id=plane_device(me, here ^ i),
            device_id_type=MESH,
        )

    def each_letter(act):
        for side in (0, 1):
            act(
                pltpu.make_async_copy(
                    mail_ref.at[here, side],
                    box_ref.at[here // 2, side, me["core"]],
                    mail_sem.at[0, 0, side],
                )
            )

        def body(i, carry):
            for side in (0, 1):
                act(letter(i, side))
            return carry

        lax.fori_loop(1, plane, body, 0)

    def copy(t, o, lane, device, own=False):
        v, first, count = trees[t][0]
        rows = pl.ds(first, count)
        spot = own_refs[v].at[o, rows]
        return pltpu.make_async_remote_copy(
            src_ref=in_refs[v].at[rows] if own else spot,
            dst_ref=spot,
            send_sem=send_sem.at[t, o, lane],
            recv_sem=recv_sem.at[t, o],
            device_id=device,
            device_id_type=MESH,
        )

    def core_copy(t, o, own=False):
        v, first, count = trees[t][0]
        rows = pl.ds(first, count)
        return pltpu.make_async_remote_copy(
            src_ref=in_refs[v].at[rows] if own else own_refs[v].at[o, rows],
            dst_ref=other_refs[v].at[o, rows],
            send_sem=core_sem.at[0, t, o],
            recv_sem=core_sem.at[1, t, o],
            device_id=moved(me, "core", 1 - me["core"]),
            device_id_type=MESH,
        )

    def flip_copy(t, o, level, own=False):
        axis = trees[t][1][level]
        return copy(t, o, 2 + level, moved(me, axis, 1 - me[axis]), own)

    count = range(len(trees))

    def sweep(act):
        for t in count:

            @pl.when(z > 0)
            def _():
                act(copy(t, mine, 0, moved(me, "z", z - 1), True))

            @pl.when(z < depth - 1)
            def _():
                act(copy(t, mine, 1, moved(me, "z", z + 1), True))

            for level in range(len(flips)):
                act(flip_copy(t, mine, level, True))
            act(core_copy(t, mine, True))

    def line(act, entering):
        for s in range(1, depth):
            for t in count:

                @pl.when(z - s >= 0)
                def _():
                    o = chip_of(me, flips, z - s, ())
                    if entering:
                        copy(t, o, 0, moved(me, "core", 1 - me["core"])).wait_recv()

                    @pl.when(z < depth - 1)
                    def _():
                        act(copy(t, o, 1, moved(me, "z", z + 1)))

                    for level in range(len(flips)):
                        act(flip_copy(t, o, level))
                    act(core_copy(t, o))

                @pl.when(z + s < depth)
                def _():
                    o = chip_of(me, flips, z + s, ())
                    if entering:
                        copy(t, o, 0, moved(me, "core", 1 - me["core"])).wait_recv()

                    @pl.when(z > 0)
                    def _():
                        act(copy(t, o, 0, moved(me, "z", z - 1)))

                    for level in range(len(flips)):
                        act(flip_copy(t, o, level))
                    act(core_copy(t, o))

    def turned_once(act, entering):
        def body(i, carry):
            for t in count:
                o = chip_of(me, flips, along(me, depth, i), trees[t][1][:1])
                if entering:
                    copy(t, o, 0, moved(me, "core", 1 - me["core"])).wait_recv()
                if len(flips) > 1:
                    act(flip_copy(t, o, 1))
                act(core_copy(t, o))
            return carry

        lax.fori_loop(0, depth, body, 0)

    def turned_last(act, entering):
        def body(i, carry):
            for some in (0, 1):
                for t in count:
                    turned = trees[t][1][1:] if some == 0 else trees[t][1]
                    o = chip_of(me, flips, along(me, depth, i), turned)
                    if entering:
                        copy(t, o, 0, moved(me, "core", 1 - me["core"])).wait_recv()
                    act(core_copy(t, o))
            return carry

        if len(flips) > 1:
            lax.fori_loop(0, depth, body, 0)

    start = lambda dma: dma.start()
    sent = lambda dma: dma.wait_send()
    sweep(start)
    if mailing:
        each_letter(start)
    line(start, True)
    turned_once(start, True)
    turned_last(start, True)
    chips = own_refs[0].shape[0]

    def arrivals(o, carry):
        for t in count:
            core_copy(t, o).wait_recv()
        return carry

    lax.fori_loop(0, chips, arrivals, 0)
    sweep(sent)
    line(sent, False)
    turned_once(sent, False)
    turned_last(sent, False)
    for local in locals_:
        local.wait()
    if mailing:
        each_letter(lambda dma: dma.wait())


def cut_rows(rows, flips, pieces):
    part = rows // pieces
    return tuple(((i * part, part), flips if i % 2 == 0 else flips[::-1]) for i in range(pieces))


def spread(values, depth, flips, ident, mail=None):
    chips = depth * 2 ** len(flips)
    trees = tuple(
        ((v,) + piece, order)
        for v, value in enumerate(values)
        for piece, order in cut_rows(value.shape[0], flips, 4 // (len(values) * len(flips) // 2 or 1))
    )
    any_space = pl.BlockSpec(memory_space=pl.ANY)
    mails = [] if mail is None else [mail]
    whole = [jax.ShapeDtypeStruct((chips,) + value.shape, value.dtype) for value in values]
    boxes = [
        jax.ShapeDtypeStruct((item.shape[0] // 2, 2, 2) + item.shape[2:], item.dtype) for item in mails
    ]
    results = whole + whole + boxes
    out = pl.pallas_call(
        functools.partial(spread_kernel, depth, trees, len(values), bool(mails)),
        out_shape=results,
        in_specs=[any_space] * (len(values) + len(mails)),
        out_specs=[any_space] * len(results),
        scratch_shapes=[
            pltpu.SemaphoreType.DMA((len(values),)),
            pltpu.SemaphoreType.DMA((len(trees), chips, 2 + len(flips))),
            pltpu.SemaphoreType.DMA((len(trees), chips)),
            pltpu.SemaphoreType.DMA((2, len(trees), chips)),
        ]
        + [pltpu.SemaphoreType.DMA((2, item.shape[0], 2)) for item in mails],
        compiler_params=pltpu.CompilerParams(collective_id=ident, has_side_effects=True),
        name="spread",
    )(*values, *mails)
    flat = [item.reshape(-1, item.shape[-1]) for item in out[: 2 * len(values)]]
    return flat, out[2 * len(values) :]


def gather_sum_kernel(depth, trees, slots, turned_rows, first_ref, second_ref, *refs):
    if slots:
        mail_ref, out_ref, box_ref, *refs = refs
    else:
        out_ref, *refs = refs
    acc, core_buf, last_buf, once_buf, line_buf, own_sem, core_sem, last_sem, once_sem, line_sem = refs[:10]
    if slots:
        slot_ref, rows_ref = first_ref, second_ref
        own_ref, (other_ref, load_buf, mail_sem) = None, refs[10:]
    else:
        own_ref, other_ref = first_ref, second_ref
    me = whereabouts()
    z = me["z"]
    flips = trees[0][1]
    every = mail_ref.shape[0] if slots else 0
    greet(me, depth, flips + ("core",), 0, every)
    count = range(len(trees))
    place = plane_index(me) // 2 * 4 + me["x"] * 2 + me["core"]

    def each_letter(act):
        act(pltpu.make_async_copy(mail_ref.at[place], box_ref.at[place], mail_sem.at[0, 0]))

        def body(i, carry):
            act(
                pltpu.make_async_remote_copy(
                    src_ref=mail_ref.at[place ^ i],
                    dst_ref=box_ref.at[place],
                    send_sem=mail_sem.at[0, i],
                    recv_sem=mail_sem.at[1, i],
                    device_id=device_at(place ^ i),
                    device_id_type=MESH,
                )
            )
            return carry

        lax.fori_loop(1, every, body, 0)

    if slots:
        each_letter(lambda dma: dma.start())
    partner = moved(me, "core", 1 - me["core"])

    def own_copy(o):
        return pltpu.make_async_copy(own_ref.at[o], acc.at[o], own_sem.at[o])

    def core_copy(o):
        return pltpu.make_async_remote_copy(
            src_ref=other_ref.at[o],
            dst_ref=core_buf.at[o],
            send_sem=core_sem.at[0, o],
            recv_sem=core_sem.at[1, o],
            device_id=partner,
            device_id_type=MESH,
        )

    def rows_of(t):
        return pl.ds(*trees[t][0])

    def flip_copy(t, o, level, place):
        axis = trees[t][1][level]
        into, sems = (once_buf, once_sem) if level == 0 else (last_buf, last_sem)
        return pltpu.make_async_remote_copy(
            src_ref=acc.at[o, rows_of(t)],
            dst_ref=into.at[t, place],
            send_sem=sems.at[0, t, place],
            recv_sem=sems.at[1, t, place],
            device_id=moved(me, axis, 1 - me[axis]),
            device_id_type=MESH,
        )

    def line_copy(t, oz, way):
        to = z + 1 if way else z - 1
        return pltpu.make_async_remote_copy(
            src_ref=acc.at[chip_of(me, flips, oz, ()), rows_of(t)],
            dst_ref=line_buf.at[t, way, oz],
            send_sem=line_sem.at[0, t, way, oz],
            recv_sem=line_sem.at[1, t, way, oz],
            device_id=moved(me, "z", to),
            device_id_type=MESH,
        )

    def add(o, rows, ref):
        first, size = rows.start, rows.size

        def body(i, carry):
            span = pl.ds(pl.multiple_of(first + i * 16, 16), 16)
            from_span = pl.ds(pl.multiple_of(i * 16, 16), 16)
            acc[o, span] = (acc[o, span].astype(F32) + ref[from_span].astype(F32)).astype(BF)
            return carry

        lax.fori_loop(0, size // 16, body, 0)

    def combos():
        first, second = flips[0], flips[-1]
        if len(flips) > 1:
            return ((first, second), (first,), (second,), ())
        return ((first,), ())

    def combine_all():
        here = rows_ref.shape[0]
        near, width = acc.shape[1:]
        part = width // 4
        pairs = acc.shape[0] // 2
        head = 2 * me["x"] + me["core"]

        def pair_at(i):
            oy = jnp.where(i < depth, 1 - me["y"], me["y"])
            return along(me, depth, depth - 1 - lax.rem(i, depth)) * 2 + oy

        def feed_pair(i):
            pair = pair_at(i)
            for aside in (True, False):
                ox = 1 - me["x"] if aside else me["x"]
                o = 2 * pair + ox
                core_copy(o).wait_recv()
                add(o, pl.ds(0, near), core_buf.at[o])
                for t in count:
                    order = trees[t][1]
                    if order[1] == "x" and aside:
                        flip_copy(t, o, 1, pair).start()
                    if order[1] == "y":

                        @pl.when(i < depth)
                        def _():
                            flip_copy(t, o, 1, pair // 2 * 2 + ox).start()

        def load(j):
            group = pair_at(j // 2) + jnp.where(lax.rem(j, 2) == 0, pairs, 0)
            slot = lax.rem(j, 2)
            span = pl.ds(pl.multiple_of(group * slots, 16), slots)
            return pltpu.make_async_copy(rows_ref.at[:, span], load_buf.at[slot], own_sem.at[slot])

        def combine(j, into):
            pair = pair_at(j // 2)
            slot = lax.rem(j, 2)
            group = pair + jnp.where(slot == 0, pairs, 0)
            places = lax.broadcasted_iota(jnp.int32, (slots, GROUP), 0)
            named = slot_ref[group]
            chosen = jnp.concatenate(
                [(places == named[e : e + 1, :]).astype(F32) for e in range(here)], axis=0
            ).astype(BF)
            rows = jnp.concatenate([load_buf[slot, e] for e in range(here)], axis=0)
            for k in range(4):
                start = pl.multiple_of((head ^ k) * part, part) if turned_rows else k * part
                block = tn(chosen, rows[:, k * part : (k + 1) * part]).astype(BF)
                into[2 * pair, :, pl.ds(start, part)] = block[:near]
                into[2 * pair + 1, :, pl.ds(start, part)] = block[near:]

        load(0).start()

        def step(i, carry):
            load(2 * i + 1).start()
            load(2 * i).wait()
            combine(2 * i, other_ref)
            core_copy(2 * pair_at(i)).start()
            core_copy(2 * pair_at(i) + 1).start()

            @pl.when(i < pairs - 1)
            def _():
                load(2 * i + 2).start()

            load(2 * i + 1).wait()
            combine(2 * i + 1, acc)

            @pl.when(i > 0)
            def _():
                feed_pair(i - 1)

            return carry

        lax.fori_loop(0, pairs, step, 0)
        feed_pair(pairs - 1)

    if slots:
        combine_all()
    else:
        for turned in combos():

            def begin(i, carry):
                o = chip_of(me, flips, along(me, depth, depth - 1 - i), turned)
                core_copy(o).start()
                own_copy(o).start()
                return carry

            lax.fori_loop(0, depth, begin, 0)

    def place_last(t, oz, first_turned):
        axis = trees[t][1][0]
        return oz * 2 + (1 - me[axis] if first_turned else me[axis])

    for turned in () if slots else combos():

        def feed(i, carry):
            oz = along(me, depth, depth - 1 - i)
            o = chip_of(me, flips, oz, turned)
            own_copy(o).wait()
            core_copy(o).wait_recv()
            add(o, pl.ds(0, acc.shape[1]), core_buf.at[o])
            for t in count:
                order = trees[t][1]
                if len(order) > 1 and order[1] in turned:
                    flip_copy(t, o, 1, place_last(t, oz, order[0] in turned)).start()
                if len(order) == 1 and order[0] in turned:
                    flip_copy(t, o, 0, oz).start()
            return carry

        lax.fori_loop(0, depth, feed, 0)

    if len(flips) > 1:

        def middle(i, carry):
            oz = along(me, depth, depth - 1 - i)
            for t in count:
                order = trees[t][1]
                o = chip_of(me, flips, oz, order[:1])
                place = place_last(t, oz, True)
                flip_copy(t, o, 1, place).wait_recv()
                add(o, rows_of(t), last_buf.at[t, place])
                flip_copy(t, o, 0, oz).start()
            return carry

        lax.fori_loop(0, depth, middle, 0)

    def settle(i, carry):
        oz = along(me, depth, depth - 1 - i)
        o = chip_of(me, flips, oz, ())
        for t in count:
            if len(flips) > 1:
                place = place_last(t, oz, False)
                flip_copy(t, o, 1, place).wait_recv()
                add(o, rows_of(t), last_buf.at[t, place])
            flip_copy(t, o, 0, oz).wait_recv()
            add(o, rows_of(t), once_buf.at[t, oz])

            @pl.when(jnp.logical_and(oz > z, z == 0))
            def _():
                line_copy(t, oz, 1).start()

            @pl.when(jnp.logical_and(oz < z, z == depth - 1))
            def _():
                line_copy(t, oz, 0).start()

        return carry

    lax.fori_loop(0, depth, settle, 0)

    for far in range(depth - 1, 0, -1):
        for t in count:
            right, left = z + far, z - far

            @pl.when(jnp.logical_and(right < depth, z > 0))
            def _():
                line_copy(t, right, 1).wait_recv()
                add(chip_of(me, flips, right, ()), rows_of(t), line_buf.at[t, 1, right])
                line_copy(t, right, 1).start()

            @pl.when(jnp.logical_and(left >= 0, z < depth - 1))
            def _():
                line_copy(t, left, 0).wait_recv()
                add(chip_of(me, flips, left, ()), rows_of(t), line_buf.at[t, 0, left])
                line_copy(t, left, 0).start()

    mine = chip_of(me, flips, z, ())
    for t in count:

        @pl.when(z > 0)
        def _():
            line_copy(t, z, 1).wait_recv()
            add(mine, rows_of(t), line_buf.at[t, 1, z])

        @pl.when(z < depth - 1)
        def _():
            line_copy(t, z, 0).wait_recv()
            add(mine, rows_of(t), line_buf.at[t, 0, z])

    out_ref[...] = acc[mine]

    def finish(o, carry):
        core_copy(o).wait_send()
        return carry

    lax.fori_loop(0, acc.shape[0], finish, 0)

    def finish_flips(oz, carry):
        for t in count:
            order = trees[t][1]
            flip_copy(t, chip_of(me, flips, oz, order[:1]), 0, oz).wait_send()
            if len(order) > 1:
                for first_turned in (False, True):
                    turned = order if first_turned else order[1:]
                    o = chip_of(me, flips, oz, turned)
                    flip_copy(t, o, 1, place_last(t, oz, first_turned)).wait_send()

            @pl.when(oz > z)
            def _():
                line_copy(t, oz, 1).wait_send()

            @pl.when(oz < z)
            def _():
                line_copy(t, oz, 0).wait_send()

        return carry

    lax.fori_loop(0, depth, finish_flips, 0)
    if slots:
        each_letter(lambda dma: dma.wait())


def gather_sum(
    depth, flips, ident, rows, own=None, other=None, slot=None, picked=None, turned=False, mail=None
):
    chips = depth * 2 ** len(flips)
    trees = cut_rows(rows, flips, 2 * len(flips))
    count, part = len(trees), trees[0][0][1]
    spots = 2 * depth if len(flips) > 1 else 1
    any_space = pl.BlockSpec(memory_space=pl.ANY)
    vmem = pl.BlockSpec(memory_space=pltpu.VMEM)
    if slot is None:
        slots, operands, width, more = 0, (own, other), own.shape[-1], []
    else:
        here, width = picked.shape[0], picked.shape[-1]
        slots, operands = picked.shape[1] // slot.shape[0], (slot, picked)
        more = [
            pltpu.VMEM((chips, rows, width), BF),
            pltpu.VMEM((2, here, slots, width), BF),
            pltpu.SemaphoreType.DMA((2, mail.shape[0])),
        ]
    mails = [] if mail is None else [mail]
    total = pl.pallas_call(
        functools.partial(gather_sum_kernel, depth, trees, slots, turned),
        out_shape=[jax.ShapeDtypeStruct((rows, width), BF)]
        + [jax.ShapeDtypeStruct(item.shape, item.dtype) for item in mails],
        in_specs=[any_space if slot is None else vmem, any_space] + [any_space] * len(mails),
        out_specs=[vmem] + [any_space] * len(mails),
        scratch_shapes=[
            pltpu.VMEM((chips, rows, width), BF),
            pltpu.VMEM((chips, rows, width), BF),
            pltpu.VMEM((count, spots, part, width), BF),
            pltpu.VMEM((count, depth, part, width), BF),
            pltpu.VMEM((count, 2, depth, part, width), BF),
            pltpu.SemaphoreType.DMA((chips,)),
            pltpu.SemaphoreType.DMA((2, chips)),
            pltpu.SemaphoreType.DMA((2, count, spots)),
            pltpu.SemaphoreType.DMA((2, count, depth)),
            pltpu.SemaphoreType.DMA((2, count, 2, depth)),
        ]
        + more,
        compiler_params=pltpu.CompilerParams(
            collective_id=ident, has_side_effects=True, vmem_limit_bytes=48 * 1024 * 1024
        ),
        name="gather_sum",
    )(*operands, *mails)
    return total if mails else total[0]


def attention_forward_kernel(scale, q_ref, k_ref, vt_ref, ot_ref, o_ref, lse_ref, s_ref):
    rows = k_ref.shape[0]
    chunk = 512
    top = None
    for c in range(rows // chunk):
        part = nt(k_ref[pl.ds(c * chunk, chunk), :], q_ref[...]) * scale
        s_ref[pl.ds(c * chunk, chunk), :] = part
        high = jnp.max(part, axis=0, keepdims=True)
        top = high if top is None else jnp.maximum(top, high)
    total = jnp.zeros_like(top)
    acc = jnp.zeros(ot_ref.shape, F32)
    for c in range(rows // chunk):
        weights = jnp.exp2(s_ref[pl.ds(c * chunk, chunk), :] - top)
        total = total + jnp.sum(weights, axis=0, keepdims=True)
        acc = acc + nn(vt_ref[:, pl.ds(c * chunk, chunk)], weights.astype(BF))
    out = acc / total
    ot_ref[...] = out.astype(BF)
    o_ref[...] = out.T.astype(BF)
    lse_ref[...] = (top + jnp.log2(total))[None]


def attention_forward(q_aug, k_aug, v_t):
    rows, deep = q_aug.shape
    block = 256
    return pl.pallas_call(
        functools.partial(attention_forward_kernel, HD ** (-0.5) * LOG2E),
        grid=(rows // block,),
        in_specs=[
            pl.BlockSpec((block, deep), lambda i: (i, 0)),
            pl.BlockSpec((rows, deep), lambda i: (0, 0)),
            pl.BlockSpec((HD, rows), lambda i: (0, 0)),
        ],
        out_specs=[
            pl.BlockSpec((HD, block), lambda i: (0, i)),
            pl.BlockSpec((block, HD), lambda i: (i, 0)),
            pl.BlockSpec((1, 1, block), lambda i: (i, 0, 0)),
        ],
        out_shape=[
            jax.ShapeDtypeStruct((HD, rows), BF),
            jax.ShapeDtypeStruct((rows, HD), BF),
            jax.ShapeDtypeStruct((rows // block, 1, block), F32),
        ],
        scratch_shapes=[pltpu.VMEM((rows, block), F32)],
        compiler_params=pltpu.CompilerParams(vmem_limit_bytes=VMEM_LIMIT),
        name="attention_forward",
    )(q_aug, k_aug, v_t)


def attention_backward_kernel(
    scale,
    q_ref,
    k_ref,
    kt_ref,
    v_ref,
    ot_ref,
    dot_ref,
    lse_ref,
    dq_ref,
    dk_ref,
    dv_ref,
    dk_acc,
    dv_acc,
):
    step = pl.program_id(0)
    rows = k_ref.shape[0]
    chunk = 512
    d_out_t = dot_ref[...]
    d_out = d_out_t.astype(F32).T.astype(BF)
    delta = jnp.sum(d_out_t.astype(F32) * ot_ref[...].astype(F32), axis=0, keepdims=True)
    lse = lse_ref[0]
    queries = q_ref[...]
    plain = queries[:, :HD]

    @pl.when(step == 0)
    def _():
        dk_acc[...] = jnp.zeros_like(dk_acc)
        dv_acc[...] = jnp.zeros_like(dv_acc)

    acc = jnp.zeros(dot_ref.shape, F32)
    for c in range(rows // chunk):
        span = pl.ds(c * chunk, chunk)
        chances = jnp.exp2(nt(k_ref[span, :], queries) * (scale * LOG2E) - lse)
        d_chances = nn(v_ref[span, :], d_out_t)
        d_scores = (chances * (d_chances - delta)).astype(BF)
        dv_acc[span, :] += nn(chances.astype(BF), d_out)
        dk_acc[span, :] += nn(d_scores, plain)
        acc = acc + nn(kt_ref[:, span], d_scores)
    dq_ref[...] = (acc * scale).T.astype(BF)

    @pl.when(step == pl.num_programs(0) - 1)
    def _():
        dk_ref[...] = (dk_acc[...] * scale).astype(BF)
        dv_ref[...] = dv_acc[...].astype(BF)


def attention_backward(q_aug, k_aug, k_t, v, o_t, d_o_t, lse):
    rows, deep = q_aug.shape
    block = 256
    whole = lambda shape: pl.BlockSpec(shape, lambda i: (0, 0))
    return pl.pallas_call(
        functools.partial(attention_backward_kernel, HD ** (-0.5)),
        grid=(rows // block,),
        in_specs=[
            pl.BlockSpec((block, deep), lambda i: (i, 0)),
            whole((rows, deep)),
            whole((HD, rows)),
            whole((rows, HD)),
            pl.BlockSpec((HD, block), lambda i: (0, i)),
            pl.BlockSpec((HD, block), lambda i: (0, i)),
            pl.BlockSpec((1, 1, block), lambda i: (i, 0, 0)),
        ],
        out_specs=[
            pl.BlockSpec((block, HD), lambda i: (i, 0)),
            whole((rows, HD)),
            whole((rows, HD)),
        ],
        out_shape=[jax.ShapeDtypeStruct((rows, HD), BF)] * 3,
        scratch_shapes=[pltpu.VMEM((rows, HD), F32)] * 2,
        compiler_params=pltpu.CompilerParams(vmem_limit_bytes=VMEM_LIMIT),
        name="attention_backward",
    )(q_aug, k_aug, k_t, v, o_t, d_o_t, lse)


STEP = 2


def slot_matrix(slot_ref, j, here, slots):
    places = lax.broadcasted_iota(jnp.int32, (slots, GROUP), 0)
    return jnp.concatenate(
        [(places == slot_ref[j, e : e + 1, :]).astype(F32) for e in range(here)], axis=0
    )


def dispatch_rows_kernel(here, slots, slot_ref, own_ref, other_ref, out_ref):
    half = pl.num_programs(0) // 2

    def place(rows_ref):
        for j in range(STEP):
            chosen = slot_matrix(slot_ref, j, here, slots).astype(BF)
            rows = nn(chosen, rows_ref[j * GROUP : (j + 1) * GROUP]).astype(BF)
            for e in range(here):
                out_ref[e, j * slots : (j + 1) * slots] = rows[e * slots : (e + 1) * slots]

    @pl.when(pl.program_id(0) < half)
    def _():
        place(own_ref)

    @pl.when(pl.program_id(0) >= half)
    def _():
        place(other_ref)


def pair_specs(half, width):
    return [
        pl.BlockSpec((STEP * GROUP, width), lambda i, *_: (jnp.minimum(i, half - 1), 0)),
        pl.BlockSpec((STEP * GROUP, width), lambda i, *_: (jnp.maximum(i - half, 0), 0)),
    ]


def dispatch_rows(slot, own, other, slots):
    groups, here, _ = slot.shape
    width = own.shape[1]
    return pl.pallas_call(
        functools.partial(dispatch_rows_kernel, here, slots),
        grid=(groups // STEP,),
        in_specs=[pl.BlockSpec((STEP, here, GROUP), lambda i: (i, 0, 0))]
        + pair_specs(groups // 2 // STEP, width),
        out_specs=pl.BlockSpec((here, STEP * slots, width), lambda i: (0, i, 0)),
        out_shape=jax.ShapeDtypeStruct((here, groups * slots, width), BF),
        compiler_params=pltpu.CompilerParams(vmem_limit_bytes=VMEM_LIMIT),
        name="dispatch_rows",
    )(slot, own, other)


def dispatch_routed_kernel(
    here, slots, head_ref, slot_ref, router_ref, own_ref, other_ref, out_ref, gate_ref
):
    half = pl.num_programs(0) // 2
    width = own_ref.shape[1]
    part = width // 4
    head = head_ref[0]

    def place(rows_ref):
        logits = nt(router_ref[...], rows_ref[...])
        odds = jnp.exp(logits - jnp.max(logits, axis=0, keepdims=True))
        probs = odds[0:8] / jnp.sum(odds, axis=0, keepdims=True)
        for j in range(STEP):
            chosen_f = slot_matrix(slot_ref, j, here, slots)
            chosen = chosen_f.astype(BF)
            cols = slice(j * GROUP, (j + 1) * GROUP)
            for e in range(here):
                weights = chosen_f[e * slots : (e + 1) * slots] * probs[e : e + 1, cols]
                gate_ref[e, j * slots : (j + 1) * slots] = jnp.sum(weights, axis=1, keepdims=True)
            for k in range(4):
                span = pl.ds(pl.multiple_of((head ^ k) * part, part), part)
                rows = nn(chosen, rows_ref[cols, span]).astype(BF)
                for e in range(here):
                    out_ref[e, j * slots : (j + 1) * slots, k * part : (k + 1) * part] = rows[
                        e * slots : (e + 1) * slots
                    ]

    @pl.when(pl.program_id(0) < half)
    def _():
        place(own_ref)

    @pl.when(pl.program_id(0) >= half)
    def _():
        place(other_ref)


def dispatch_routed(head, slot, router_t, own, other, slots):
    groups, here, _ = slot.shape
    width = own.shape[1]
    return pl.pallas_call(
        functools.partial(dispatch_routed_kernel, here, slots),
        grid_spec=pltpu.PrefetchScalarGridSpec(
            num_scalar_prefetch=1,
            grid=(groups // STEP,),
            in_specs=[
                pl.BlockSpec((STEP, here, GROUP), lambda i, *_: (i, 0, 0)),
                pl.BlockSpec(router_t.shape, lambda i, *_: (0, 0)),
            ]
            + pair_specs(groups // 2 // STEP, width),
            out_specs=[
                pl.BlockSpec((here, STEP * slots, width), lambda i, *_: (0, i, 0)),
                pl.BlockSpec((here, STEP * slots, 1), lambda i, *_: (0, i, 0)),
            ],
        ),
        out_shape=[
            jax.ShapeDtypeStruct((here, groups * slots, width), BF),
            jax.ShapeDtypeStruct((here, groups * slots, 1), F32),
        ],
        compiler_params=pltpu.CompilerParams(vmem_limit_bytes=VMEM_LIMIT),
        name="dispatch_routed",
    )(head, slot, router_t, own, other)


def experts_kernel(
    place_ref,
    x_ref,
    g_ref,
    gate_ref,
    a0,
    a1,
    a2,
    a3,
    p1,
    p2,
    p3,
    low_own,
    low_other,
    d_pre_ref,
    weighted_ref,
    d_gate_ref,
    y_ref,
    dx_ref,
):
    parts = (p1, p2, p3)
    own = (a0, a1, a2, a3)
    depth = p1.shape[1]
    half = p1.shape[2] // 2
    quarter = low_own.shape[1]
    first = x_ref[0, :, :depth]
    pre = jnp.concatenate([nn(first, a[0]) for a in own], axis=1)
    for k, p in enumerate(parts, 1):
        pre = pre + nn(x_ref[0, :, k * depth : (k + 1) * depth], p[0])
    gate_pre, up_pre = pre[:, :half], pre[:, half:]
    sigmoid = jax.nn.sigmoid(gate_pre)
    swished = gate_pre * sigmoid
    hidden = (swished * up_pre).astype(BF)
    d_raw = jnp.concatenate([nt(g_ref[0], low_own[0]), nt(g_ref[0], low_other[0])], axis=1)
    gate = gate_ref[0]
    d_gate_ref[0] = jnp.sum(hidden.astype(F32) * d_raw, axis=1, keepdims=True)
    d_hidden = d_raw * gate
    d_gate_pre = (d_hidden * up_pre * (sigmoid * (1.0 + gate_pre * (1.0 - sigmoid)))).astype(BF)
    d_up_pre = (d_hidden * swished).astype(BF)
    weighted = (hidden.astype(F32) * gate).astype(BF)
    weighted_ref[0] = weighted
    d_pre_ref[0, :, :half] = d_gate_pre
    d_pre_ref[0, :, half:] = d_up_pre
    y = nn(weighted[:, :quarter], low_own[0]) + nn(weighted[:, quarter:], low_other[0])
    y_ref[0] = y.astype(BF)
    dx = nt(d_gate_pre[:, :quarter], a0[0]) + nt(d_gate_pre[:, quarter:], a1[0])
    dx = dx + nt(d_up_pre[:, :quarter], a2[0]) + nt(d_up_pre[:, quarter:], a3[0])
    dx_ref[0, :, :depth] = dx.astype(BF)
    for k, p in enumerate(parts, 1):
        dx = nt(d_gate_pre, p[0, :, :half]) + nt(d_up_pre, p[0, :, half:])
        dx_ref[0, :, k * depth : (k + 1) * depth] = dx.astype(BF)


def run_experts(place, x_rows, g_rows, gate_rows, w_gate, w_up, parts, w_down, low_other):
    here, slots, width = x_rows.shape
    depth, both = parts[0].shape[1:]
    quarter = low_other.shape[1]
    tile = 256
    row = lambda n: pl.BlockSpec((1, tile, n), lambda e, m, _: (e, m, 0))
    weight = lambda a, b: pl.BlockSpec((1, a, b), lambda e, m, _: (e, 0, 0))
    mine = lambda r: pl.BlockSpec(
        (1, depth, quarter), lambda e, m, p: (p[1] * here + e, 0, 2 * p[0] + (r ^ p[1]))
    )
    sizes = ((both, BF), (both // 2, BF), (1, F32), (width, BF), (width, BF))
    return pl.pallas_call(
        experts_kernel,
        grid_spec=pltpu.PrefetchScalarGridSpec(
            num_scalar_prefetch=1,
            grid=(here, slots // tile),
            in_specs=[row(width), row(width), row(1)]
            + [mine(0), mine(1)] * 2
            + [weight(depth, both)] * 3
            + [
                pl.BlockSpec((1, quarter, width), lambda e, m, p: (p[1] * here + e, 0, 0)),
                weight(quarter, width),
            ],
            out_specs=[row(n) for n, _ in sizes],
        ),
        out_shape=[jax.ShapeDtypeStruct((here, slots, n), kind) for n, kind in sizes],
        compiler_params=pltpu.CompilerParams(vmem_limit_bytes=VMEM_LIMIT),
        name="run_experts",
    )(place, x_rows, g_rows, gate_rows, w_gate, w_gate, w_up, w_up, *parts, w_down, low_other)


def expert_grads_kernel(place_ref, x_ref, g_ref, d_pre_ref, weighted_ref, q0, q1, q2, q3, own_ref, send_ref):
    depth = q0.shape[1]
    quarter = own_ref.shape[1]
    d_pre = d_pre_ref[0]
    for k, q in enumerate((q0, q1, q2, q3)):
        q[0] = tn(x_ref[0, :, k * depth : (k + 1) * depth], d_pre).astype(BF)
    g = g_ref[0]
    own_ref[0] = tn(weighted_ref[0, :, :quarter], g)
    send_ref[0] = tn(weighted_ref[0, :, quarter:], g).astype(BF)


def expert_grads(place, x_rows, g_rows, d_pre, weighted):
    here, slots, width = x_rows.shape
    both = d_pre.shape[2]
    quarter = both // 4
    block = lambda a, b: pl.BlockSpec((1, a, b), lambda e, _: (e, 0, 0))
    return pl.pallas_call(
        expert_grads_kernel,
        grid_spec=pltpu.PrefetchScalarGridSpec(
            num_scalar_prefetch=1,
            grid=(here,),
            in_specs=[
                block(slots, width),
                block(slots, width),
                block(slots, both),
                block(slots, both // 2),
            ],
            out_specs=[block(width // 4, both)] * 4
            + [
                pl.BlockSpec((1, quarter, width), lambda e, p: (p[1] * here + e, 0, 0)),
                block(quarter, width),
            ],
        ),
        out_shape=[jax.ShapeDtypeStruct((here, width // 4, both), BF)] * 4
        + [
            jax.ShapeDtypeStruct((2 * here, quarter, width), F32),
            jax.ShapeDtypeStruct((here, quarter, width), BF),
        ],
        compiler_params=pltpu.CompilerParams(vmem_limit_bytes=VMEM_LIMIT),
        name="expert_grads",
    )(place, x_rows, g_rows, d_pre, weighted)


def place_in_kernel(spots, place_ref, *refs):
    gate_ref, up_ref = refs[len(spots) :]
    group, side, e = pl.program_id(0), pl.program_id(1), pl.program_id(2)
    piece = 2 * (side ^ place_ref[0]) + (group ^ place_ref[1])
    quarter = gate_ref.shape[2] // 2
    for (k, first, count), p in zip(spots, refs):

        @pl.when((piece == k) & (e >= first) & (e < first + count))
        def _():
            for r in (0, 1):
                span = pl.ds(pl.multiple_of((r ^ group) * quarter, quarter), quarter)
                gate_ref[0, :, span] = p[0, :, r * quarter : (r + 1) * quarter].astype(F32)
                up_ref[0, :, span] = p[0, :, (2 + r) * quarter : (3 + r) * quarter].astype(F32)


def place_in(place, here, pieces):
    depth, both = pieces[0][1].shape[1:]
    spots = tuple(key + (value.shape[0],) for key, value in pieces)

    def piece_spec(k, first, count):
        def index(group, side, e, place_ref):
            chosen = 2 * (side ^ place_ref[0]) + (group ^ place_ref[1]) == k
            return (jnp.where(chosen, jnp.clip(e - first, 0, count - 1), 0), 0, 0)

        return pl.BlockSpec((1, depth, both), index)

    out = pl.BlockSpec((1, depth, both // 2), lambda group, side, e, _: (group * here + e, 0, side))
    return pl.pallas_call(
        functools.partial(place_in_kernel, spots),
        grid_spec=pltpu.PrefetchScalarGridSpec(
            num_scalar_prefetch=1,
            grid=(2, 2, here),
            in_specs=[piece_spec(*spot) for spot in spots],
            out_specs=[out, out],
        ),
        out_shape=[jax.ShapeDtypeStruct((2 * here, depth, both), F32)] * 2,
        compiler_params=pltpu.CompilerParams(vmem_limit_bytes=VMEM_LIMIT),
        name="place_in",
    )(place, *(value for _, value in pieces))


def place_low_kernel(place_ref, full_ref, got_ref, out_ref):
    out_ref[...] = got_ref[...].astype(F32)


def place_low(place, full, got):
    here, quarter, width = got.shape
    block = (1, quarter, width)
    return pl.pallas_call(
        place_low_kernel,
        grid_spec=pltpu.PrefetchScalarGridSpec(
            num_scalar_prefetch=1,
            grid=(here,),
            in_specs=[
                pl.BlockSpec(memory_space=pl.ANY),
                pl.BlockSpec(block, lambda e, _: (e, 0, 0)),
            ],
            out_specs=pl.BlockSpec(block, lambda e, p: ((1 - p[1]) * here + e, 0, 0)),
        ),
        out_shape=jax.ShapeDtypeStruct(full.shape, F32),
        input_output_aliases={1: 0},
        compiler_params=pltpu.CompilerParams(vmem_limit_bytes=VMEM_LIMIT),
        name="place_low",
    )(place, full, got)


def fast_device(
    tokens,
    cotangent,
    lengths,
    routes,
    attn_gain,
    w_query,
    w_key,
    w_value,
    w_out,
    ffn_gain,
    w_router,
    w_gate,
    w_up,
    w_down,
):
    _, sub_rows, width = tokens.shape
    held, part, hidden_width = w_gate.shape
    here = held // 2
    half_hidden = hidden_width // 2
    x, core = lax.axis_index("x"), lax.axis_index("core")
    block = lax.axis_index(("z", "y"))
    blocks = width // sub_rows // 4
    head = 2 * x + core
    head_id = 2 * block + core
    place = jnp.stack([x, core]).astype(jnp.int32)
    head_vec = jnp.reshape(head, (1,)).astype(jnp.int32)
    near = 2 * sub_rows

    gains = to_everyone(jnp.stack([attn_gain, ffn_gain]), ALL, 4 * blocks)
    gains = gains.transpose(1, 0, 2).reshape(2, width).astype(F32)
    qkv_cols = jnp.stack([w_query, w_key, w_value], axis=1).reshape(sub_rows, 3, HEADS, HD)
    qkv_cols = qkv_cols.transpose(2, 0, 1, 3).reshape(HEADS, sub_rows, 3 * HD)
    sheet = jnp.concatenate(
        [w_router, routes.transpose(1, 0, 2).reshape(sub_rows, 2 * TOP).astype(BF)], axis=1
    )
    sheet = jnp.pad(sheet, ((0, 0), (0, HD - E - 2 * TOP)))

    def piece_of(k):
        to_x, to_core = x ^ (k >> 1), core ^ (k & 1)
        size = (here, part, half_hidden // 2)
        return jnp.concatenate(
            [
                lax.dynamic_slice(
                    w, (here * to_core, 0, half_hidden * to_x + size[2] * (r ^ to_core)), size
                )
                for w in (w_gate, w_up)
                for r in (0, 1)
            ],
            axis=2,
        )

    down_halves = w_down.reshape((2, here) + w_down.shape[1:])
    outgoing = [piece_of(k) for k in (1, 2, 3)] + [pick(down_halves, 1 - core)]
    wo_cols = lax.all_to_all(w_out, "core", split_axis=1, concat_axis=0, tiled=True)
    got = [swap_x(pick(tokens, 1 - x)), swap_x(qkv_cols), swap_x(sheet), swap_x(wo_cols)]
    outgoing, got, gains = lax.optimization_barrier((outgoing, got, gains))
    gain_one_f, gain_two_f = gains[0], gains[1]
    tok_m = in_order(x, pick(tokens, x), got[0]).astype(F32)
    inverse_one = lax.rsqrt(jnp.mean(tok_m * tok_m, axis=-1, keepdims=True) + epsilon)
    normed_one = tok_m * inverse_one
    act_one = (normed_one * gain_one_f).astype(BF)
    mail = in_order(x, qkv_cols[:, None], got[1][:, None], axis=1)
    sheet = in_order(x, sheet[None], got[2][None])
    mail = jnp.concatenate(
        [mail, jnp.broadcast_to(sheet[None], (HEADS, 2, sub_rows, HD))], axis=3
    )
    w_parts = [swap_head(outgoing[k - 1], k) for k in (1, 2, 3)]
    low_other = swap_core(outgoing[3])
    (act_own, wo_own, act_other, wo_other), (box,) = spread(
        [act_one, in_order(x, wo_cols, got[3])], blocks // 2, ("y",), 1, mail=mail
    )
    act_own, act_other, box, w_parts[0], low_other = lax.optimization_barrier(
        (act_own, act_other, box, w_parts[0], low_other)
    )
    w_qkv = box[..., : 3 * HD].reshape(width, 3 * HD)
    router_full = box[..., 3 * HD : 3 * HD + E].reshape(width, E)
    routes_seen = box[..., 3 * HD + E : 3 * HD + E + 2 * TOP].astype(jnp.int32)
    routes_seen = routes_seen.reshape(blocks, 2, 2, sub_rows, 2, TOP).transpose(2, 0, 4, 1, 3, 5)
    routes_seen = routes_seen.reshape(2, -1, TOP)
    routes_seen = in_order(core, routes_seen[0], routes_seen[1])
    groups = routes_seen.shape[0] // GROUP
    slots = (GROUP // sub_rows) * MOST
    my_experts = held * block + here * core + jnp.arange(here, dtype=jnp.int32)
    named = jnp.any(routes_seen[:, None, :] == my_experts[None, :, None], axis=-1)
    named = named.reshape(groups, GROUP, here).transpose(0, 2, 1)
    ranking = jnp.cumsum(named.astype(jnp.int32), axis=2) - 1
    slot = jnp.where(named, ranking, -1)
    router_t = jnp.roll(router_full.T, -(held * block + here * core), axis=0)

    qkv = in_order(core, nn(act_own, w_qkv).astype(BF), nn(act_other, w_qkv).astype(BF))
    rows = qkv.shape[0]
    order = jnp.arange(rows, dtype=jnp.int32).reshape(2, blocks, 2, sub_rows)
    position = (
        jnp.arange(2, dtype=jnp.int32)[:, None, None, None] * sub_rows
        + jnp.arange(blocks, dtype=jnp.int32)[None, :, None, None] * (4 * sub_rows)
        + jnp.arange(2, dtype=jnp.int32)[None, None, :, None] * near
        + jnp.arange(sub_rows, dtype=jnp.int32)
    ).reshape(order.size)
    live = position < pick(lengths, x)
    bias = jnp.where(live, 0.0, big_negative).astype(BF)[:, None]
    q, k, v = qkv[:, :HD], qkv[:, HD : 2 * HD], qkv[:, 2 * HD :]
    q_aug = jnp.concatenate([q, jnp.ones((rows, HD), BF)], axis=1)
    k_aug = jnp.concatenate([k, bias, jnp.zeros((rows, HD - 1), BF)], axis=1)
    o_t, attended, lse = attention_forward(q_aug, k_aug, v.T)

    att = attended.reshape(2, blocks, near, HD).transpose(1, 0, 2, 3).reshape(HEADS, near, HD)
    att = lax.all_to_all(att, HEAD_AXES, split_axis=0, concat_axis=0, tiled=True)
    att = att.transpose(1, 0, 2).reshape(near, width)
    resid = tok_m + in_order(core, nn(att, wo_own), nn(att, wo_other), axis=1)
    inverse_two = lax.rsqrt(jnp.mean(resid * resid, axis=-1, keepdims=True) + epsilon)
    normed_two = resid * inverse_two
    act_two = (normed_two * gain_two_f).astype(BF)

    cot_b = cotangent.astype(BF).reshape(near, width)
    (two_own, cot_own, two_other, cot_other), _ = spread(
        [act_two, cot_b], blocks // 2, ("y", "x"), 2
    )
    slot_raw = slot.reshape(groups, here, 2, 2, sub_rows).swapaxes(2, 3).reshape(slot.shape)
    g_rows = dispatch_rows(slot_raw, cot_own, cot_other, slots)
    probs = jax.nn.softmax(nn(act_two, router_full), axis=-1)
    x_rows, gate_rows = dispatch_routed(head_vec, slot, router_t, two_own, two_other, slots)

    d_pre, weighted, d_gate_rows, y_rows, d_x_rows = run_experts(
        place, x_rows, g_rows, gate_rows, w_gate, w_up, w_parts, w_down, low_other
    )
    *grad_pieces, low_grad, low_send = expert_grads(place, x_rows, g_rows, d_pre, weighted)

    chosen = jnp.arange(slots, dtype=jnp.int32)[None, None, :, None] == slot[:, :, None, :]
    d_gate_slots = d_gate_rows.reshape(here, groups, slots).transpose(1, 0, 2)
    d_probs_seen = jnp.sum(jnp.where(chosen, d_gate_slots[..., None], 0.0), axis=2)
    d_probs_seen = (
        d_probs_seen.reshape(2, groups // 2, here, GROUP // near, near)
        .transpose(0, 1, 3, 2, 4)
        .reshape(2, groups // 2 * (GROUP // near), here, near)
    )
    d_probs_seen = in_order(core, d_probs_seen[0:1], d_probs_seen[1:2]).transpose(1, 0, 2, 3)
    d_probs_seen = d_probs_seen.reshape(-1, here, near)
    depth = blocks // 2
    d_probs_seen = jnp.pad(d_probs_seen, ((0, 0), (0, 8 - here), (0, 0)))
    d_act_routes, d_probs = gather_sum(
        depth, ("y", "x"), 3, near, slot=slot, picked=d_x_rows, turned=True, mail=d_probs_seen
    )

    d_act_routes, y_rows, low_send, grad_pieces = lax.optimization_barrier(
        (d_act_routes, y_rows, low_send, grad_pieces)
    )
    pieces = [grad_pieces[0], swap_head(grad_pieces[1], 1), None, swap_head(grad_pieces[3], 3)]
    cot_m = to_middle(cotangent, x)
    low_got = swap_core(low_send)

    d_probs = jnp.sum(d_probs[:, :here].reshape(blocks, 2, 2 * here, near), axis=1)
    d_probs = d_probs.reshape(E, near).T

    d_logits = (probs * (d_probs - jnp.sum(probs * d_probs, axis=-1, keepdims=True))).astype(BF)
    grad_router = tn(act_two, d_logits)
    d_act_two = d_act_routes.astype(F32) + nt(d_logits, router_full)
    grad_gain_two = jnp.sum(d_act_two * normed_two, axis=0)
    d_resid = cot_m + norm_backward(d_act_two * gain_two_f, normed_two, inverse_two)
    d_attn = d_resid.astype(BF)

    (d_attn_own, d_attn_other), _ = spread([d_attn], blocks // 2, ("y",), 5)
    d_attn_own, d_attn_other, across = lax.optimization_barrier(
        (d_attn_own, d_attn_other, grad_pieces[2])
    )
    pieces[2] = swap_head(across, 2)
    wo_rows = in_order(
        core,
        lax.dynamic_slice_in_dim(wo_own, head_id * HD, HD),
        lax.dynamic_slice_in_dim(wo_other, head_id * HD, HD),
        axis=1,
    )
    d_o_t = in_order(
        core, nt(wo_rows, d_attn_own).astype(BF), nt(wo_rows, d_attn_other).astype(BF), axis=1
    )
    dq, dk, dv = attention_backward(q_aug, k_aug, k.T, v, o_t, d_o_t, lse)
    d_qkv = jnp.concatenate([dq, dk, dv], axis=1)

    half_rows = rows // 2
    d_halves = d_qkv.reshape(2, half_rows, 3 * HD)
    d_one_other = nt(pick(d_halves, 1 - core), w_qkv).astype(BF)
    d_one_own = nt(pick(d_halves, core), w_qkv).astype(BF)
    d_one_own, d_one_other, pieces[3] = lax.optimization_barrier(
        (d_one_own, d_one_other, pieces[3])
    )
    d_act_one = gather_sum(
        depth,
        ("y",),
        4,
        near,
        own=d_one_own.reshape(-1, near, width),
        other=d_one_other.reshape(-1, near, width),
    )
    grad_qkv = tn(act_own, pick(d_halves, core)) + tn(act_other, pick(d_halves, 1 - core))
    y_rows, d_act_one, pieces[2] = lax.optimization_barrier((y_rows, d_act_one, pieces[2]))
    d_act_one = d_act_one.astype(F32)

    o_halves = o_t.reshape(HD, 2, half_rows)
    o_own = lax.dynamic_index_in_dim(o_halves, core, 1, keepdims=False)
    o_other = lax.dynamic_index_in_dim(o_halves, 1 - core, 1, keepdims=False)
    grad_wo_rows = nn(o_own, d_attn_own) + nn(o_other, d_attn_other)
    wo_send = jnp.where(
        (jnp.arange(4, dtype=jnp.int32) // 2 == core)[:, None, None],
        jnp.concatenate([grad_wo_rows, grad_wo_rows], axis=0).reshape(4, sub_rows, width),
        0.0,
    )

    grad_gain_one = jnp.sum(d_act_one * normed_one, axis=0)
    grad_tok_m = d_resid + norm_backward(d_act_one * gain_one_f, normed_one, inverse_one)
    grad_tokens = from_middle(grad_tok_m, x)

    owners = 4 * blocks
    letters = jnp.concatenate(
        [
            grad_qkv.astype(BF),
            grad_router.astype(BF),
            grad_gain_one[:, None].astype(BF),
            grad_gain_two[:, None].astype(BF),
            jnp.zeros((width, HD - E - 2), BF),
        ],
        axis=1,
    ).reshape(owners, sub_rows, 4 * HD)
    moe, box = gather_sum(depth, ("y", "x"), 6, near, slot=slot, picked=y_rows, mail=letters)
    moe, box, wo_send = lax.optimization_barrier((moe, box, wo_send))
    output = from_middle((resid + moe.astype(F32)).astype(BF), x)
    part_wo = sum_to_owners(wo_send.reshape(4 * sub_rows, width).astype(BF), ("x", "core"), 4)
    box = box.reshape(blocks, 2, 2, sub_rows, 4 * HD).astype(F32)
    grad_qkv = jnp.sum(box[..., : 3 * HD], axis=1).reshape(HEADS, sub_rows, 3, HD)
    grad_qkv = grad_qkv.transpose(2, 1, 0, 3).reshape(3, sub_rows, width)
    rest = jnp.sum(box[..., 3 * HD :], axis=(0, 1, 2))
    router_part, gain_part = rest[:, :E], rest[:, E : E + 2].T

    grad_gate, grad_up = place_in(place, here, [((k, 0), piece) for k, piece in enumerate(pieces)])
    grad_down = place_low(place, low_grad, low_got)

    return (
        output,
        grad_tokens,
        gain_part[0],
        grad_qkv[0],
        grad_qkv[1],
        grad_qkv[2],
        part_wo,
        gain_part[1],
        router_part,
        grad_gate,
        grad_up,
        grad_down,
    )


def solution(mesh):
    blk, head = mesh.shape["blk"], mesh.shape["head"]
    fast = blk * head == 2 * HEADS and head == 4 and E % (2 * blk) == 0

    def specs(every, blocks, heads):
        rows = P(None, every, None)
        flat = P(every)
        table = P(every, None)
        expert = P(blocks, heads, None)
        placed = (rows, rows, P(), rows, flat, table, table, table, table, flat, table)
        given = (rows, rows, flat, table, table, table, table, flat, table)
        return placed + (expert,) * 3, given + (expert,) * 3

    if fast:
        devices = mesh.devices.reshape(blk // 2, 2, 2, 2)
        mesh_four = Mesh(devices, ALL)
        placed, given = specs(ALL, ("z", "y"), ("x", "core"))
        return jax.shard_map(
            fast_device, mesh=mesh_four, in_specs=placed, out_specs=given, check_vma=False
        )
    placed, given = specs(("blk", "head"), "blk", "head")
    return jax.shard_map(
        general_device, mesh=mesh, in_specs=placed, out_specs=given, check_vma=False
    )
```

profile of v0, /device:TPU:10, one launch (start us, length us, event | category | flops | bytes accessed | tf_op | source)
XLA Modules:
  0.0 1000.7 jit_solution(873674856442635411)
XLA Ops:
  4.5 4.1 all-to-all-start
  10.9 6.0 all-to-all-start.1
  28.2 5.4 constant_dynamic-slice_fusion.7
  45.2 3.0 collective-permute-done.1
  66.3 125.1 %spread.3 = (bf16[8,128,2048]{2,1,0:T(8,128)(2,1)}, bf16[8,256,1024]{2,1,0:T(8,128)(2,1)}, bf16[8,128,2048]{2,1,0:T(8,128)(2,1)}, bf16[8,256,1024]{2,1,0:T(8,128)(2,1)}, bf16[8,2,2,64,512]{4,3,2,1,0:T(8,128)(2,1)}) custom-call(bf16[128,2048]{1,0:T(8,128)(2,1)} %fusion.7.refs_0_, bf16[256,1024]{1,0:T(8,128)(2,1)} %maximum_select_fusion.6.refs_1_, ...), custom_call_target="tpu_custom_call" | custom-call | tf_op jit(solution)/shard_map/spread/pallas_call | solution.py:723
  198.5 4.7 convolution_convert_fusion.3
  220.5 13.3 %attention_forward.1 = (bf16[128,2048]{1,0:T(8,128)(2,1)}, bf16[2048,128]{1,0:T(8,128)(2,1)}, f32[8,1,256]{2,1,0:T(1,128)}) custom-call(bf16[2048,256]{1,0:T(8,128)(2,1)} %slice_select_fusion.q_ref, bf16[2048,256]{1,0:T(8,128)(2,1)} %maximum_maximum_fusion.k_ref, bf16[128,2048]{1,0:T(8,128)(2,1)} %copy.169.vt_ref), custom_call_target="tpu_custom_call" | custom-call | tf_op jit(solution)/shard_map/attention_forward/pallas_call | solution.py:1120
  235.7 4.6 all-to-all-start.2
  247.3 6.7 all-to-all-done.2
  254.2 3.1 fusion.49
  260.0 144.7 %spread.4 = (bf16[16,128,2048]{2,1,0:T(8,128)(2,1)}, bf16[16,128,2048]{2,1,0:T(8,128)(2,1)}, bf16[16,128,2048]{2,1,0:T(8,128)(2,1)}, bf16[16,128,2048]{2,1,0:T(8,128)(2,1)}) custom-call(bf16[128,2048]{1,0:T(8,128)(2,1)} %multiply_convert_fusion.refs_0_, bf16[128,2048]{1,0:T(8,128)(2,1)} %bitcast.209), custom_call_target="tpu_custom_call" | custom-call | tf_op jit(solution)/shard_map/spread/pallas_call | solution.py:723
  404.7 14.1 %dispatch_rows.1.g_ref = bf16[4,768,2048]{2,1,0:T(8,128)(2,1)} custom-call(s32[16,4,256]{2,1,0:T(4,128)} %reshape.436.slot_ref, bf16[2048,2048]{1,0:T(8,128)(2,1)} %bitcast.187, bf16[2048,2048]{1,0:T(8,128)(2,1)} %bitcast.188), custom_call_target="tpu_custom_call" | custom-call | tf_op jit(solution)/shard_map/dispatch_rows/pallas_call | solution.py:1258
  418.8 17.4 %dispatch_routed.1 = (bf16[4,768,2048]{2,1,0:T(8,128)(2,1)}, f32[4,768,1]{2,1,0:T(8,128)}) custom-call(s32[1]{0:T(128)} %bitcast.39.head_ref, s32[16,4,256]{2,1,0:T(4,128)} %copy-done.1, bf16[64,2048]{1,0:T(8,128)(2,1)} %fusion.21.router_ref, bf16[2048,2048]{1,0:T(8,128)(2,1)} %bitcast.189, bf16[2048,2048]{1,0:T(8,128)(2,1)} %bitcast.190), custom_call_target="tpu_custom_call" | custom-call | tf_op jit(solution)/shard_map/dispatch_routed/pallas_call | solution.py:1309
  436.6 51.2 %run_experts.1 = (bf16[4,768,1024]{2,1,0:T(8,128)(2,1)}, bf16[4,768,512]{2,1,0:T(8,128)(2,1)}, f32[4,768,1]{2,1,0:T(8,128)}, bf16[4,768,2048]{2,1,0:T(8,128)(2,1)}, bf16[4,768,2048]{2,1,0:T(8,128)(2,1)}) custom-call(s32[2]{0:T(128)} %pad_add_fusion.place_ref, bf16[4,768,2048]{2,1,0:T(8,128)(2,1)} %get-tuple-element.99.x_ref, ...), custom_call_target="tpu_custom_call" | custom-call | tf_op jit(solution)/shard_map/run_experts/pallas_call | solution.py:1397
  490.6 105.1 %gather_sum.3 = (bf16[128,2048]{1,0:T(8,128)(2,1)S(1)}, f32[32,8,128]{2,1,0:T(8,128)S(1)}) custom-call(s32[16,4,256]{2,1,0:T(4,128)S(1)} %copy-done.2, bf16[4,768,2048]{2,1,0:T(8,128)(2,1)} %get-tuple-element.107.second_ref, f32[32,8,128]{2,1,0:T(8,128)S(1)} %pad.10.refs_0_), custom_call_target="tpu_custom_call" | custom-call | tf_op jit(solution)/shard_map/gather_sum/pallas_call | solution.py:1069
  595.9 26.6 %expert_grads.1 = (bf16[4,512,1024]{2,1,0:T(8,128)(2,1)}, bf16[4,512,1024]{2,1,0:T(8,128)(2,1)}, bf16[4,512,1024]{2,1,0:T(8,128)(2,1)}, bf16[4,512,1024]{2,1,0:T...) custom-call(s32[2]{0:T(128)} %pad_add_fusion.place_ref, ...), custom_call_target="tpu_custom_call" | custom-call | tf_op jit(solution)/shard_map/expert_grads/pallas_call | solution.py:1433
  624.3 2.8 fusion.39
  627.1 52.2 %spread.5 = (bf16[8,128,2048]{2,1,0:T(8,128)(2,1)}, bf16[8,128,2048]{2,1,0:T(8,128)(2,1)}) custom-call(bf16[128,2048]{1,0:T(8,128)(2,1)} %get-tuple-element.156.refs_0_), custom_call_target="tpu_custom_call" | custom-call | tf_op jit(solution)/shard_map/spread/pallas_call | solution.py:723
  680.4 4.0 convolution_convert_fusion.6
  686.9 16.4 %attention_backward.1 = (bf16[2048,128]{1,0:T(8,128)(2,1)}, bf16[2048,128]{1,0:T(8,128)(2,1)}, bf16[2048,128]{1,0:T(8,128)(2,1)}) custom-call(bf16[2048,256]{1,0:T(8,128)(2,1)} %slice_select_fusion.q_ref, bf16[2048,256]{1,0:T(8,128)(2,1)} %maximum_maximum_fusion.k_ref, bf16[128,2048]{1,0:T(8,128)(2,1)} %copy.183.kt_ref, ...), custom_call_target="tpu_custom_call" | custom-call | tf_op jit(solution)/shard_map/attention_backward/pallas_call | solution.py:1195
  703.4 3.1 fusion.22
  708.4 4.4 convolution_convert_fusion.1
  712.8 4.4 convolution_convert_fusion
  717.2 4.0 fusion.12
  725.6 7.1 add_convert_fusion
  732.7 75.9 %gather_sum.4 = bf16[128,2048]{1,0:T(8,128)(2,1)S(1)} custom-call(bf16[8,128,2048]{2,1,0:T(8,128)(2,1)S(1)} %bitcast.183, bf16[8,128,2048]{2,1,0:T(8,128)(2,1)} %bitcast.206), custom_call_target="tpu_custom_call" | custom-call | tf_op jit(solution)/shard_map/gather_sum/pallas_call | solution.py:1069
  811.8 4.5 concatenate.179.refs_0_
  816.4 122.9 %gather_sum.5 = (bf16[128,2048]{1,0:T(8,128)(2,1)S(1)}, bf16[32,64,512]{2,1,0:T(8,128)(2,1)S(1)}) custom-call(s32[16,4,256]{2,1,0:T(4,128)S(1)} %copy-done.2, bf16[4,768,2048]{2,1,0:T(8,128)(2,1)} %get-tuple-element.135.second_ref, bf16[32,64,512]{2,1,0:T(8,128)(2,1)S(1)} %concatenate.179.refs_0_), custom_call_target="tpu_custom_call" | custom-call | tf_op jit(solution)/shard_map/gather_sum/pallas_call | solution.py:1069
  940.6 5.2 all-to-all-start.3
  956.9 2.5 reshape.453
  964.8 6.6 place_low.1
  972.8 21.5 %place_in.1 = (f32[8,512,1024]{2,1,0:T(8,128)}, f32[8,512,1024]{2,1,0:T(8,128)}) custom-call(s32[2]{0:T(128)} %pad_add_fusion.place_ref, bf16[4,512,1024]{2,1,0:T(8,128)(2,1)} %get-tuple-element.142.refs_0_, bf16[4,512,1024]{2,1,0:T(8,128)(2,1)} %collective-permute-done.13.refs_1_, bf16[4,512,1024]{2,1,0:T(8,128)(2,1)} %collective-permute-done.10.refs_2_, ...), custom_call_target="tpu_custom_call" | custom-call | tf_op jit(solution)/shard_map/place_in/pallas_call | solution.py:1487
  (263 shorter events, 126.2 us)
Async XLA Ops:
  2.3 42.9 %collective-permute-start.2 = (bf16[64,128]{1,0:T(8,128)(2,1)S(1)}, bf16[64,128]{1,0:T(8,128)(2,1)S(1)}, u32[]{:S(2)}, u32[]{:S(2)}) collective-permute-start(bf16[64,128]{1,0:T(8,128)(2,1)S(1)} %fusion.31), channel_id=1, source_target_pairs={{0,2},{2,0},{1,3},{3,1},{4,6},{6,4},{5,7},{7,5},{8,10},{10,8},{9,1... | collective-permute-start | bytes 49160 | tf_op jit(solution)/shard_map/ppermute | solution.py:393
  4.5 5.8 all-to-all-start
  10.9 34.1 %all-to-all-start.1 = ((bf16[32,2,64]{2,1,0:T(2,128)(2,1)}), bf16[32,2,64]{2,1,0:T(2,128)(2,1)S(1)}, u32[]{:S(2)}, u32[]{:S(2)}) async-start(bf16[32,2,64]{2,1,0:T(2,128)(2,1)} %broadcast_in_dim.44), calls=%async_computation.1 | async-start | bytes 32768 | tf_op jit(solution)/shard_map/all_to_all | solution.py:418
  17.0 28.2 %collective-permute-start.3 = (bf16[128,1024]{1,0:T(8,128)(2,1)}, bf16[128,1024]{1,0:T(8,128)(2,1)}, u32[]{:S(2)}, u32[]{:S(2)}) collective-permute-start(bf16[128,1024]{1,0:T(8,128)(2,1)} %bitcast.8), channel_id=1, source_target_pairs={{0,2},{2,0},{1,3},{3,1},{4,6},{6,4},{5,7},{7,5},{8,10},{10,8},{9,1... | collective-permute-start | bytes 786440 | tf_op jit(solution)/shard_map/ppermute | solution.py:393
  19.4 25.8 %collective-permute-start = (bf16[64,2048]{1,0:T(8,128)(2,1)}, bf16[64,2048]{1,0:T(8,128)(2,1)S(1)}, u32[]{:S(2)}, u32[]{:S(2)}) collective-permute-start(bf16[64,2048]{1,0:T(8,128)(2,1)} %get-tuple-element.188), channel_id=1, source_target_pairs={{0,2},{2,0},{1,3},{3,1},{4,6},{6,4},{5,7},{7,5},{8,10},{10,8},{9,1... | collective-permute-start | bytes 786440 | tf_op jit(solution)/shard_map/ppermute | solution.py:393
  27.6 20.6 %collective-permute-start.1 = (bf16[16,64,384]{2,1,0:T(8,128)(2,1)}, bf16[16,64,384]{2,1,0:T(8,128)(2,1)}, u32[]{:S(2)}, u32[]{:S(2)}) collective-permute-start(bf16[16,64,384]{2,1,0:T(8,128)(2,1)} %reshape.417), channel_id=1, source_target_pairs={{0,2},{2,0},{1,3},{3,1},{4,6},{6,4},{5,7},{7,5},{8,10},{10,8},{9,1... | collective-permute-start | bytes 2359304 | tf_op jit(solution)/shard_map/ppermute | solution.py:393
  45.2 763.4 %copy-start.8 = (bf16[64,2048]{1,0:T(8,128)(2,1)}, bf16[64,2048]{1,0:T(8,128)(2,1)S(1)}, u32[]{:S(2)}) copy-start(bf16[64,2048]{1,0:T(8,128)(2,1)S(1)} %collective-permute-done) | copy-start | bytes 786436
  48.2 146.5 %collective-permute-start.4 = (bf16[4,512,1024]{2,1,0:T(8,128)(2,1)}, bf16[4,512,1024]{2,1,0:T(8,128)(2,1)}, u32[]{:S(2)}, u32[]{:S(2)}) collective-permute-start(bf16[4,512,1024]{2,1,0:T(8,128)(2,1)} %pad_maximum_fusion), channel_id=1, source_target_pairs={{0,1},{1,0},{2,3},{3,2},{4,5},{5,4},{6,7},{7,6},{8,9},{9,8},{10,11... | collective-permute-start | bytes 12582920 | tf_op jit(solution)/shard_map/ppermute | solution.py:401
  48.2 146.5 %collective-permute-start.5 = (bf16[4,256,2048]{2,1,0:T(8,128)(2,1)}, bf16[4,256,2048]{2,1,0:T(8,128)(2,1)}, u32[]{:S(2)}, u32[]{:S(2)}) collective-permute-start(bf16[4,256,2048]{2,1,0:T(8,128)(2,1)} %dynamic-slice_bitcast_fusion), channel_id=1, source_target_pairs={{0,1},{1,0},{2,3},{3,2},{4,5},{5,4},{6,7},{7,6},{8,9},{9,8},{10,11... | collective-permute-start | bytes 12582920 | tf_op jit(solution)/shard_map/ppermute | solution.py:397
  49.8 574.5 %collective-permute-start.8 = (f32[64,2048]{1,0:T(8,128)}, f32[64,2048]{1,0:T(8,128)}, u32[]{:S(2)}, u32[]{:S(2)}) collective-permute-start(f32[64,2048]{1,0:T(8,128)} %get-tuple-element.181), channel_id=1, source_target_pairs={{0,2},{2,0},{1,3},{3,1},{4,6},{6,4},{5,7},{7,5},{8,10},{10,8},{9,1... | collective-permute-start | bytes 1572872 | tf_op jit(solution)/shard_map/ppermute | solution.py:393
  57.4 379.2 %collective-permute-start.6 = (bf16[4,512,1024]{2,1,0:T(8,128)(2,1)}, bf16[4,512,1024]{2,1,0:T(8,128)(2,1)}, u32[]{:S(2)}, u32[]{:S(2)}) collective-permute-start(bf16[4,512,1024]{2,1,0:T(8,128)(2,1)} %pad_maximum_fusion.1), channel_id=1, source_target_pairs={{0,2},{1,3},{2,0},{3,1},{4,6},{5,7},{6,4},{7,5},{8,10},{9,11},{10,... | collective-permute-start | bytes 12582920 | tf_op jit(solution)/shard_map/ppermute | solution.py:401
  58.8 377.8 %collective-permute-start.7 = (bf16[4,512,1024]{2,1,0:T(8,128)(2,1)}, bf16[4,512,1024]{2,1,0:T(8,128)(2,1)}, u32[]{:S(2)}, u32[]{:S(2)}) collective-permute-start(bf16[4,512,1024]{2,1,0:T(8,128)(2,1)} %pad_maximum_fusion.2), channel_id=1, source_target_pairs={{0,3},{1,2},{2,1},{3,0},{4,7},{5,6},{6,5},{7,4},{8,11},{9,10},{10,... | collective-permute-start | bytes 12582920 | tf_op jit(solution)/shard_map/ppermute | solution.py:401
  64.7 133.0 %copy-start.36 = (f32[128]{0:T(128)}, f32[128]{0:T(128)S(1)}, u32[]{:S(2)}) copy-start(f32[128]{0:T(128)S(1)} %add_rsqrt_fusion.1) | copy-start | bytes 1540
  65.3 130.7 %copy-start.31 = (f32[1,2048]{1,0:T(1,128)}, f32[1,2048]{1,0:T(1,128)S(1)}, u32[]{:S(2)}) copy-start(f32[1,2048]{1,0:T(1,128)S(1)} %get-tuple-element.194) | copy-start | bytes 24580
  218.7 23.2 %copy-start.16 = (bf16[128,2048]{0,1:T(8,128)(2,1)S(1)}, bf16[128,2048]{0,1:T(8,128)(2,1)}, u32[]{:S(2)}) copy-start(bf16[128,2048]{0,1:T(8,128)(2,1)} %get-tuple-element.176) | copy-start | bytes 1572868
  235.7 18.3 %all-to-all-start.2 = ((bf16[16,128,128]{2,1,0:T(8,128)(2,1)}), bf16[16,128,128]{2,1,0:T(8,128)(2,1)S(1)}, u32[]{:S(2)}, u32[]{:S(2)}) async-start(bf16[16,128,128]{2,1,0:T(8,128)(2,1)} %bitcast.26), calls=%async_computation.2 | async-start | bytes 1048576 | tf_op jit(solution)/shard_map/all_to_all | solution.py:1633
  258.8 365.5 %copy-start.5 = (f32[128,2048]{1,0:T(8,128)}, f32[128,2048]{1,0:T(8,128)S(1)}, u32[]{:S(2)}) copy-start(f32[128,2048]{1,0:T(8,128)S(1)} %get-tuple-element.159) | copy-start | bytes 3145732
  436.6 53.2 %copy-start.2 = (s32[16,4,256]{2,1,0:T(4,128)S(1)}, s32[16,4,256]{2,1,0:T(4,128)}, u32[]{:S(2)}) copy-start(s32[16,4,256]{2,1,0:T(4,128)} %copy-done.1) | copy-start | bytes 196612
  595.8 28.5 %copy-start.18 = (f32[64,2048]{1,0:T(8,128)S(1)}, f32[64,2048]{1,0:T(8,128)}, u32[]{:S(2)}) copy-start(f32[64,2048]{1,0:T(8,128)} %get-tuple-element.182) | copy-start | bytes 1572868
  622.4 58.0 %copy-start.28 = (bf16[128,1024]{1,0:T(8,128)(2,1)S(1)}, bf16[128,1024]{1,0:T(8,128)(2,1)}, u32[]{:S(2)}) copy-start(bf16[128,1024]{1,0:T(8,128)(2,1)} %constant_dynamic-slice_fusion.5) | copy-start | bytes 786436
  622.4 110.2 %collective-permute-start.9 = (bf16[4,512,1024]{2,1,0:T(8,128)(2,1)}, bf16[4,512,1024]{2,1,0:T(8,128)(2,1)}, u32[]{:S(2)}, u32[]{:S(2)}) collective-permute-start(bf16[4,512,1024]{2,1,0:T(8,128)(2,1)} %get-tuple-element.131), channel_id=1, source_target_pairs={{0,3},{1,2},{2,1},{3,0},{4,7},{5,6},{6,5},{7,4},{8,11},{9,10},{10,... | collective-permute-start | bytes 12582920 | tf_op jit(solution)/shard_map/ppermute | solution.py:401
  622.5 350.2 %collective-permute-start.13 = (bf16[4,512,1024]{2,1,0:T(8,128)(2,1)}, bf16[4,512,1024]{2,1,0:T(8,128)(2,1)}, u32[]{:S(2)}, u32[]{:S(2)}) collective-permute-start(bf16[4,512,1024]{2,1,0:T(8,128)(2,1)} %get-tuple-element.143), channel_id=1, source_target_pairs={{0,1},{1,0},{2,3},{3,2},{4,5},{5,4},{6,7},{7,6},{8,9},{9,8},{10,11... | collective-permute-start | bytes 12582920 | tf_op jit(solution)/shard_map/ppermute | solution.py:401
  623.7 341.1 %collective-permute-start.14 = (bf16[4,256,2048]{2,1,0:T(8,128)(2,1)}, bf16[4,256,2048]{2,1,0:T(8,128)(2,1)}, u32[]{:S(2)}, u32[]{:S(2)}) collective-permute-start(bf16[4,256,2048]{2,1,0:T(8,128)(2,1)} %get-tuple-element.149), channel_id=1, source_target_pairs={{0,1},{1,0},{2,3},{3,2},{4,5},{5,4},{6,7},{7,6},{8,9},{9,8},{10,11... | collective-permute-start | bytes 12582920 | tf_op jit(solution)/shard_map/ppermute | solution.py:397
  627.1 57.4 %copy-start.29 = (bf16[128,1024]{1,0:T(8,128)(2,1)S(1)}, bf16[128,1024]{1,0:T(8,128)(2,1)}, u32[]{:S(2)}) copy-start(bf16[128,1024]{1,0:T(8,128)(2,1)} %constant_dynamic-slice_fusion.4) | copy-start | bytes 786436
  679.3 129.2 %collective-permute-start.10 = (bf16[4,512,1024]{2,1,0:T(8,128)(2,1)}, bf16[4,512,1024]{2,1,0:T(8,128)(2,1)}, u32[]{:S(2)}, u32[]{:S(2)}) collective-permute-start(bf16[4,512,1024]{2,1,0:T(8,128)(2,1)} %get-tuple-element.134), channel_id=1, source_target_pairs={{0,2},{1,3},{2,0},{3,1},{4,6},{5,7},{6,4},{7,5},{8,10},{9,11},{10,... | collective-permute-start | bytes 12582920 | tf_op jit(solution)/shard_map/ppermute | solution.py:401
  732.7 75.9 %copy-start.32 = (f32[1,2048]{1,0:T(1,128)S(1)}, f32[1,2048]{1,0:T(1,128)}, u32[]{:S(2)}) copy-start(f32[1,2048]{1,0:T(1,128)} %copy-done.31) | copy-start | bytes 24580
  732.7 75.9 %copy-start.37 = (f32[128]{0:T(128)S(1)}, f32[128]{0:T(128)}, u32[]{:S(2)}) copy-start(f32[128]{0:T(128)} %copy-done.36) | copy-start | bytes 1540
  732.7 79.2 %copy-start.17 = (bf16[2048,64]{1,0:T(8,128)(2,1)S(1)}, bf16[2048,64]{1,0:T(8,128)(2,1)}, u32[]{:S(2)}) copy-start(bf16[2048,64]{1,0:T(8,128)(2,1)} %copy.184) | copy-start | bytes 786436
  940.6 58.7 %all-to-all-start.3 = ((bf16[4,64,2048]{2,1,0:T(8,128)(2,1)}), bf16[4,64,2048]{2,1,0:T(8,128)(2,1)S(1)}, u32[]{:S(2)}, u32[]{:S(2)}) async-start(bf16[4,64,2048]{2,1,0:T(8,128)(2,1)} %broadcast_select_fusion), calls=%async_computation.3 | async-start | bytes 2097152 | tf_op jit(solution)/shard_map/all_to_all | solution.py:423
  948.1 47.0 %collective-permute-start.11 = (bf16[64,2048]{1,0:T(8,128)(2,1)}, bf16[64,2048]{1,0:T(8,128)(2,1)}, u32[]{:S(2)}, u32[]{:S(2)}) collective-permute-start(bf16[64,2048]{1,0:T(8,128)(2,1)} %get-tuple-element.184), channel_id=1, source_target_pairs={{0,2},{2,0},{1,3},{3,1},{4,6},{6,4},{5,7},{7,5},{8,10},{10,8},{9,1... | collective-permute-start | bytes 786440 | tf_op jit(solution)/shard_map/ppermute | solution.py:393
  950.8 46.2 %collective-permute-start.12 = (f32[64,2048]{1,0:T(8,128)}, f32[64,2048]{1,0:T(8,128)}, u32[]{:S(2)}, u32[]{:S(2)}) collective-permute-start(f32[64,2048]{1,0:T(8,128)} %get-tuple-element.180), channel_id=1, source_target_pairs={{0,2},{2,0},{1,3},{3,1},{4,6},{6,4},{5,7},{7,5},{8,10},{10,8},{9,1... | collective-permute-start | bytes 1572872 | tf_op jit(solution)/shard_map/ppermute | solution.py:393
  972.7 24.3 %copy-start.15 = (f32[1,64,2048]{2,1,0:T(8,128)S(1)}, f32[1,64,2048]{2,1,0:T(8,128)}, u32[]{:S(2)}) copy-start(f32[1,64,2048]{2,1,0:T(8,128)} %get-tuple-element.179) | copy-start | bytes 1572868
  (31 other events, 258.8 us)
where the time goes:
time: 1010 us; the launch traced here: 1000 us
  Pallas kernels  793 us (79%)
  local copies, waits for them, and re-layouts  70 us (7%)
  other arithmetic  53.7 us (5%)
  matrix products  41.2 us (4%)
  starting transfers between devices  30.1 us (3%)
  waiting for transfers between devices  10.7 us (1%)
    pallas_call x3, Pallas kernels, spread(): pl.pallas_call(functools.partial(spread_kernel, depth, trees, len(values)...  322 us
    pallas_call x3, Pallas kernels, gather_sum(): pl.pallas_call(functools.partial(gather_sum_kernel, depth, trees, slots,...  304 us
    pallas_call x1, Pallas kernels, run_experts(): pl.pallas_call(experts_kernel, grid_spec=pltpu.PrefetchScalarGridSpec(num...  51.2 us
    pallas_call x1, Pallas kernels, expert_grads(): pl.pallas_call(expert_grads_kernel, grid_spec=pltpu.PrefetchScalarGridSpe...  26.6 us
    pallas_call x1, Pallas kernels, place_in(): pl.pallas_call(functools.partial(place_in_kernel, spots), grid_spec=pltpu...  21.5 us
  transfers between devices with their start and end apart: 19, of which 3 were waited for; matrix products, arithmetic and copies ran while one was open for 16% of the time, Pallas kernels for 79%

commit v1 on v0

--- a/solution.py
+++ b/solution.py
@@ -1216,7 +1216,7 @@
     )(q_aug, k_aug, k_t, v, o_t, d_o_t, lse)
 
 
-STEP = 2
+STEP = 4
 
 
 def slot_matrix(slot_ref, j, here, slots):
@@ -1387,7 +1387,7 @@
     here, slots, width = x_rows.shape
     depth, both = parts[0].shape[1:]
     quarter = low_other.shape[1]
-    tile = 256
+    tile = 384
     row = lambda n: pl.BlockSpec((1, tile, n), lambda e, m, _: (e, m, 0))
     weight = lambda a, b: pl.BlockSpec((1, a, b), lambda e, m, _: (e, 0, 0))
     mine = lambda r: pl.BlockSpec(
@@ -1457,45 +1457,49 @@
     )(place, x_rows, g_rows, d_pre, weighted)
 
 
-def place_in_kernel(spots, place_ref, *refs):
-    gate_ref, up_ref = refs[len(spots) :]
-    group, side, e = pl.program_id(0), pl.program_id(1), pl.program_id(2)
+def place_in_kernel(place_ref, *refs):
+    gate_ref, up_ref = refs[4:]
+    group, side = pl.program_id(0), pl.program_id(1)
     piece = 2 * (side ^ place_ref[0]) + (group ^ place_ref[1])
     quarter = gate_ref.shape[2] // 2
-    for (k, first, count), p in zip(spots, refs):
-
-        @pl.when((piece == k) & (e >= first) & (e < first + count))
+    for k, p in enumerate(refs[:4]):
+
+        @pl.when(piece == k)
         def _():
             for r in (0, 1):
                 span = pl.ds(pl.multiple_of((r ^ group) * quarter, quarter), quarter)
-                gate_ref[0, :, span] = p[0, :, r * quarter : (r + 1) * quarter].astype(F32)
-                up_ref[0, :, span] = p[0, :, (2 + r) * quarter : (3 + r) * quarter].astype(F32)
-
-
-def place_in(place, here, pieces):
-    depth, both = pieces[0][1].shape[1:]
-    spots = tuple(key + (value.shape[0],) for key, value in pieces)
-
-    def piece_spec(k, first, count):
+                for j in range(gate_ref.shape[0]):
+                    gate_ref[j, :, span] = p[j, :, r * quarter : (r + 1) * quarter].astype(F32)
+                    up_ref[j, :, span] = p[j, :, (2 + r) * quarter : (3 + r) * quarter].astype(F32)
+
+
+def place_in(place, pieces):
+    here, depth, both = pieces[0].shape
+    some = 2
+    steps = here // some
+
+    def piece_spec(k):
         def index(group, side, e, place_ref):
             chosen = 2 * (side ^ place_ref[0]) + (group ^ place_ref[1]) == k
-            return (jnp.where(chosen, jnp.clip(e - first, 0, count - 1), 0), 0, 0)
-
-        return pl.BlockSpec((1, depth, both), index)
-
-    out = pl.BlockSpec((1, depth, both // 2), lambda group, side, e, _: (group * here + e, 0, side))
+            return (jnp.where(chosen, e, 0), 0, 0)
+
+        return pl.BlockSpec((some, depth, both), index)
+
+    out = pl.BlockSpec(
+        (some, depth, both // 2), lambda group, side, e, _: (group * steps + e, 0, side)
+    )
     return pl.pallas_call(
-        functools.partial(place_in_kernel, spots),
+        place_in_kernel,
         grid_spec=pltpu.PrefetchScalarGridSpec(
             num_scalar_prefetch=1,
-            grid=(2, 2, here),
-            in_specs=[piece_spec(*spot) for spot in spots],
+            grid=(2, 2, steps),
+            in_specs=[piece_spec(k) for k in range(4)],
             out_specs=[out, out],
         ),
         out_shape=[jax.ShapeDtypeStruct((2 * here, depth, both), F32)] * 2,
         compiler_params=pltpu.CompilerParams(vmem_limit_bytes=VMEM_LIMIT),
         name="place_in",
-    )(place, *(value for _, value in pieces))
+    )(place, *pieces)
 
 
 def place_low_kernel(place_ref, full_ref, got_ref, out_ref):
@@ -1755,7 +1759,7 @@
     rest = jnp.sum(box[..., 3 * HD :], axis=(0, 1, 2))
     router_part, gain_part = rest[:, :E], rest[:, E : E + 2].T
 
-    grad_gate, grad_up = place_in(place, here, [((k, 0), piece) for k, piece in enumerate(pieces)])
+    grad_gate, grad_up = place_in(place, pieces)
     grad_down = place_low(place, low_grad, low_got)
 
     return (

time: 1010 us -> 1010 us (level)
  no operation moved by 1% of the time
where the time goes in v1:
time: 1010 us; the launch traced here: 997 us
  Pallas kernels  790 us (78%)
  local copies, waits for them, and re-layouts  70 us (7%)
  other arithmetic  53.7 us (5%)
  matrix products  41.2 us (4%)
  starting transfers between devices  30 us (3%)
  waiting for transfers between devices  10.7 us (1%)
    pallas_call x3, Pallas kernels, spread(): pl.pallas_call(functools.partial(spread_kernel, depth, trees, len(values)...  322 us
    pallas_call x3, Pallas kernels, gather_sum(): pl.pallas_call(functools.partial(gather_sum_kernel, depth, trees, slots,...  304 us
    pallas_call x1, Pallas kernels, run_experts(): pl.pallas_call(experts_kernel, grid_spec=pltpu.PrefetchScalarGridSpec(num...  50 us
    pallas_call x1, Pallas kernels, expert_grads(): pl.pallas_call(expert_grads_kernel, grid_spec=pltpu.PrefetchScalarGridSpe...  26.6 us
    pallas_call x1, Pallas kernels, place_in(): pl.pallas_call(place_in_kernel, grid_spec=pltpu.PrefetchScalarGridSpec(nu...  21.1 us
  transfers between devices with their start and end apart: 19, of which 3 were waited for; matrix products, arithmetic and copies ran while one was open for 16% of the time, Pallas kernels for 79%

profile of v1, /device:TPU:10, one launch (start us, length us, event | category | flops | bytes accessed | tf_op | source)
XLA Modules:
  0.0 997.4 jit_solution(3444506340804785920)
XLA Ops:
  4.5 4.1 all-to-all-start
  10.9 6.0 all-to-all-start.1
  28.2 5.4 constant_dynamic-slice_fusion.7
  45.2 3.0 collective-permute-done.1
  66.3 125.0 %spread.3 = (bf16[8,128,2048]{2,1,0:T(8,128)(2,1)}, bf16[8,256,1024]{2,1,0:T(8,128)(2,1)}, bf16[8,128,2048]{2,1,0:T(8,128)(2,1)}, bf16[8,256,1024]{2,1,0:T(8,128)(2,1)}, bf16[8,2,2,64,512]{4,3,2,1,0:T(8,128)(2,1)}) custom-call(bf16[128,2048]{1,0:T(8,128)(2,1)} %fusion.7.refs_0_, bf16[256,1024]{1,0:T(8,128)(2,1)} %maximum_select_fusion.6.refs_1_, ...), custom_call_target="tpu_custom_call" | custom-call | tf_op jit(solution)/shard_map/spread/pallas_call | solution.py:723
  198.5 4.7 convolution_convert_fusion.3
  220.5 13.3 %attention_forward.1 = (bf16[128,2048]{1,0:T(8,128)(2,1)}, bf16[2048,128]{1,0:T(8,128)(2,1)}, f32[8,1,256]{2,1,0:T(1,128)}) custom-call(bf16[2048,256]{1,0:T(8,128)(2,1)} %slice_select_fusion.q_ref, bf16[2048,256]{1,0:T(8,128)(2,1)} %maximum_maximum_fusion.k_ref, bf16[128,2048]{1,0:T(8,128)(2,1)} %copy.169.vt_ref), custom_call_target="tpu_custom_call" | custom-call | tf_op jit(solution)/shard_map/attention_forward/pallas_call | solution.py:1120
  235.7 4.6 all-to-all-start.2
  247.3 6.7 all-to-all-done.2
  254.2 3.1 fusion.49
  259.9 144.7 %spread.4 = (bf16[16,128,2048]{2,1,0:T(8,128)(2,1)}, bf16[16,128,2048]{2,1,0:T(8,128)(2,1)}, bf16[16,128,2048]{2,1,0:T(8,128)(2,1)}, bf16[16,128,2048]{2,1,0:T(8,128)(2,1)}) custom-call(bf16[128,2048]{1,0:T(8,128)(2,1)} %multiply_convert_fusion.refs_0_, bf16[128,2048]{1,0:T(8,128)(2,1)} %bitcast.209), custom_call_target="tpu_custom_call" | custom-call | tf_op jit(solution)/shard_map/spread/pallas_call | solution.py:723
  404.7 12.7 %dispatch_rows.1.g_ref = bf16[4,768,2048]{2,1,0:T(8,128)(2,1)} custom-call(s32[16,4,256]{2,1,0:T(4,128)} %reshape.436.slot_ref, bf16[2048,2048]{1,0:T(8,128)(2,1)} %bitcast.187, bf16[2048,2048]{1,0:T(8,128)(2,1)} %bitcast.188), custom_call_target="tpu_custom_call" | custom-call | tf_op jit(solution)/shard_map/dispatch_rows/pallas_call | solution.py:1258
  417.4 17.5 %dispatch_routed.1 = (bf16[4,768,2048]{2,1,0:T(8,128)(2,1)}, f32[4,768,1]{2,1,0:T(8,128)}) custom-call(s32[1]{0:T(128)} %bitcast.39.head_ref, s32[16,4,256]{2,1,0:T(4,128)} %copy-done.1, bf16[64,2048]{1,0:T(8,128)(2,1)} %fusion.21.router_ref, bf16[2048,2048]{1,0:T(8,128)(2,1)} %bitcast.189, bf16[2048,2048]{1,0:T(8,128)(2,1)} %bitcast.190), custom_call_target="tpu_custom_call" | custom-call | tf_op jit(solution)/shard_map/dispatch_routed/pallas_call | solution.py:1309
  435.3 50.0 %run_experts.1 = (bf16[4,768,1024]{2,1,0:T(8,128)(2,1)}, bf16[4,768,512]{2,1,0:T(8,128)(2,1)}, f32[4,768,1]{2,1,0:T(8,128)}, bf16[4,768,2048]{2,1,0:T(8,128)(2,1)}, bf16[4,768,2048]{2,1,0:T(8,128)(2,1)}) custom-call(s32[2]{0:T(128)} %pad_add_fusion.place_ref, bf16[4,768,2048]{2,1,0:T(8,128)(2,1)} %get-tuple-element.99.x_ref, ...), custom_call_target="tpu_custom_call" | custom-call | tf_op jit(solution)/shard_map/run_experts/pallas_call | solution.py:1397
  488.1 104.8 %gather_sum.3 = (bf16[128,2048]{1,0:T(8,128)(2,1)S(1)}, f32[32,8,128]{2,1,0:T(8,128)S(1)}) custom-call(s32[16,4,256]{2,1,0:T(4,128)S(1)} %copy-done.2, bf16[4,768,2048]{2,1,0:T(8,128)(2,1)} %get-tuple-element.107.second_ref, f32[32,8,128]{2,1,0:T(8,128)S(1)} %pad.10.refs_0_), custom_call_target="tpu_custom_call" | custom-call | tf_op jit(solution)/shard_map/gather_sum/pallas_call | solution.py:1069
  593.1 26.6 %expert_grads.1 = (bf16[4,512,1024]{2,1,0:T(8,128)(2,1)}, bf16[4,512,1024]{2,1,0:T(8,128)(2,1)}, bf16[4,512,1024]{2,1,0:T(8,128)(2,1)}, bf16[4,512,1024]{2,1,0:T...) custom-call(s32[2]{0:T(128)} %pad_add_fusion.place_ref, ...), custom_call_target="tpu_custom_call" | custom-call | tf_op jit(solution)/shard_map/expert_grads/pallas_call | solution.py:1433
  621.6 2.8 fusion.39
  624.4 52.2 %spread.5 = (bf16[8,128,2048]{2,1,0:T(8,128)(2,1)}, bf16[8,128,2048]{2,1,0:T(8,128)(2,1)}) custom-call(bf16[128,2048]{1,0:T(8,128)(2,1)} %get-tuple-element.156.refs_0_), custom_call_target="tpu_custom_call" | custom-call | tf_op jit(solution)/shard_map/spread/pallas_call | solution.py:723
  677.7 4.1 convolution_convert_fusion.6
  684.2 16.6 %attention_backward.1 = (bf16[2048,128]{1,0:T(8,128)(2,1)}, bf16[2048,128]{1,0:T(8,128)(2,1)}, bf16[2048,128]{1,0:T(8,128)(2,1)}) custom-call(bf16[2048,256]{1,0:T(8,128)(2,1)} %slice_select_fusion.q_ref, bf16[2048,256]{1,0:T(8,128)(2,1)} %maximum_maximum_fusion.k_ref, bf16[128,2048]{1,0:T(8,128)(2,1)} %copy.183.kt_ref, ...), custom_call_target="tpu_custom_call" | custom-call | tf_op jit(solution)/shard_map/attention_backward/pallas_call | solution.py:1195
  700.9 3.1 fusion.22
  705.9 4.4 convolution_convert_fusion.1
  710.3 4.4 convolution_convert_fusion
  714.7 4.0 fusion.12
  723.0 7.1 add_convert_fusion
  730.2 75.8 %gather_sum.4 = bf16[128,2048]{1,0:T(8,128)(2,1)S(1)} custom-call(bf16[8,128,2048]{2,1,0:T(8,128)(2,1)S(1)} %bitcast.183, bf16[8,128,2048]{2,1,0:T(8,128)(2,1)} %bitcast.206), custom_call_target="tpu_custom_call" | custom-call | tf_op jit(solution)/shard_map/gather_sum/pallas_call | solution.py:1069
  809.2 4.5 concatenate.179.refs_0_
  813.7 123.0 %gather_sum.5 = (bf16[128,2048]{1,0:T(8,128)(2,1)S(1)}, bf16[32,64,512]{2,1,0:T(8,128)(2,1)S(1)}) custom-call(s32[16,4,256]{2,1,0:T(4,128)S(1)} %copy-done.2, bf16[4,768,2048]{2,1,0:T(8,128)(2,1)} %get-tuple-element.135.second_ref, bf16[32,64,512]{2,1,0:T(8,128)(2,1)S(1)} %concatenate.179.refs_0_), custom_call_target="tpu_custom_call" | custom-call | tf_op jit(solution)/shard_map/gather_sum/pallas_call | solution.py:1069
  938.0 5.1 all-to-all-start.3
  954.3 2.5 reshape.453
  962.2 6.6 place_low.1
  970.1 21.1 %place_in.1 = (f32[8,512,1024]{2,1,0:T(8,128)}, f32[8,512,1024]{2,1,0:T(8,128)}) custom-call(s32[2]{0:T(128)} %pad_add_fusion.place_ref, bf16[4,512,1024]{2,1,0:T(8,128)(2,1)} %get-tuple-element.142.refs_0_, bf16[4,512,1024]{2,1,0:T(8,128)(2,1)} %collective-permute-done.13.refs_1_, bf16[4,512,1024]{2,1,0:T(8,128)(2,1)} %collective-permute-done.10.refs_2_, ...), custom_call_target="tpu_custom_call" | custom-call | tf_op jit(solution)/shard_map/place_in/pallas_call | solution.py:1491
  (263 shorter events, 126.1 us)
Async XLA Ops:
  2.3 42.9 %collective-permute-start.2 = (bf16[64,128]{1,0:T(8,128)(2,1)S(1)}, bf16[64,128]{1,0:T(8,128)(2,1)S(1)}, u32[]{:S(2)}, u32[]{:S(2)}) collective-permute-start(bf16[64,128]{1,0:T(8,128)(2,1)S(1)} %fusion.31), channel_id=1, source_target_pairs={{0,2},{2,0},{1,3},{3,1},{4,6},{6,4},{5,7},{7,5},{8,10},{10,8},{9,1... | collective-permute-start | bytes 49160 | tf_op jit(solution)/shard_map/ppermute | solution.py:393
  4.5 5.8 all-to-all-start
  10.9 34.1 %all-to-all-start.1 = ((bf16[32,2,64]{2,1,0:T(2,128)(2,1)}), bf16[32,2,64]{2,1,0:T(2,128)(2,1)S(1)}, u32[]{:S(2)}, u32[]{:S(2)}) async-start(bf16[32,2,64]{2,1,0:T(2,128)(2,1)} %broadcast_in_dim.44), calls=%async_computation.1 | async-start | bytes 32768 | tf_op jit(solution)/shard_map/all_to_all | solution.py:418
  17.0 28.2 %collective-permute-start.3 = (bf16[128,1024]{1,0:T(8,128)(2,1)}, bf16[128,1024]{1,0:T(8,128)(2,1)}, u32[]{:S(2)}, u32[]{:S(2)}) collective-permute-start(bf16[128,1024]{1,0:T(8,128)(2,1)} %bitcast.8), channel_id=1, source_target_pairs={{0,2},{2,0},{1,3},{3,1},{4,6},{6,4},{5,7},{7,5},{8,10},{10,8},{9,1... | collective-permute-start | bytes 786440 | tf_op jit(solution)/shard_map/ppermute | solution.py:393
  19.4 25.8 %collective-permute-start = (bf16[64,2048]{1,0:T(8,128)(2,1)}, bf16[64,2048]{1,0:T(8,128)(2,1)S(1)}, u32[]{:S(2)}, u32[]{:S(2)}) collective-permute-start(bf16[64,2048]{1,0:T(8,128)(2,1)} %get-tuple-element.188), channel_id=1, source_target_pairs={{0,2},{2,0},{1,3},{3,1},{4,6},{6,4},{5,7},{7,5},{8,10},{10,8},{9,1... | collective-permute-start | bytes 786440 | tf_op jit(solution)/shard_map/ppermute | solution.py:393
  27.6 20.6 %collective-permute-start.1 = (bf16[16,64,384]{2,1,0:T(8,128)(2,1)}, bf16[16,64,384]{2,1,0:T(8,128)(2,1)}, u32[]{:S(2)}, u32[]{:S(2)}) collective-permute-start(bf16[16,64,384]{2,1,0:T(8,128)(2,1)} %reshape.417), channel_id=1, source_target_pairs={{0,2},{2,0},{1,3},{3,1},{4,6},{6,4},{5,7},{7,5},{8,10},{10,8},{9,1... | collective-permute-start | bytes 2359304 | tf_op jit(solution)/shard_map/ppermute | solution.py:393
  45.2 760.7 %copy-start.8 = (bf16[64,2048]{1,0:T(8,128)(2,1)}, bf16[64,2048]{1,0:T(8,128)(2,1)S(1)}, u32[]{:S(2)}) copy-start(bf16[64,2048]{1,0:T(8,128)(2,1)S(1)} %collective-permute-done) | copy-start | bytes 786436
  48.2 146.4 %collective-permute-start.4 = (bf16[4,512,1024]{2,1,0:T(8,128)(2,1)}, bf16[4,512,1024]{2,1,0:T(8,128)(2,1)}, u32[]{:S(2)}, u32[]{:S(2)}) collective-permute-start(bf16[4,512,1024]{2,1,0:T(8,128)(2,1)} %pad_maximum_fusion), channel_id=1, source_target_pairs={{0,1},{1,0},{2,3},{3,2},{4,5},{5,4},{6,7},{7,6},{8,9},{9,8},{10,11... | collective-permute-start | bytes 12582920 | tf_op jit(solution)/shard_map/ppermute | solution.py:401
  48.2 146.4 %collective-permute-start.5 = (bf16[4,256,2048]{2,1,0:T(8,128)(2,1)}, bf16[4,256,2048]{2,1,0:T(8,128)(2,1)}, u32[]{:S(2)}, u32[]{:S(2)}) collective-permute-start(bf16[4,256,2048]{2,1,0:T(8,128)(2,1)} %dynamic-slice_bitcast_fusion), channel_id=1, source_target_pairs={{0,1},{1,0},{2,3},{3,2},{4,5},{5,4},{6,7},{7,6},{8,9},{9,8},{10,11... | collective-permute-start | bytes 12582920 | tf_op jit(solution)/shard_map/ppermute | solution.py:397
  49.8 571.8 %collective-permute-start.8 = (f32[64,2048]{1,0:T(8,128)}, f32[64,2048]{1,0:T(8,128)}, u32[]{:S(2)}, u32[]{:S(2)}) collective-permute-start(f32[64,2048]{1,0:T(8,128)} %get-tuple-element.181), channel_id=1, source_target_pairs={{0,2},{2,0},{1,3},{3,1},{4,6},{6,4},{5,7},{7,5},{8,10},{10,8},{9,1... | collective-permute-start | bytes 1572872 | tf_op jit(solution)/shard_map/ppermute | solution.py:393
  57.4 377.9 %collective-permute-start.6 = (bf16[4,512,1024]{2,1,0:T(8,128)(2,1)}, bf16[4,512,1024]{2,1,0:T(8,128)(2,1)}, u32[]{:S(2)}, u32[]{:S(2)}) collective-permute-start(bf16[4,512,1024]{2,1,0:T(8,128)(2,1)} %pad_maximum_fusion.1), channel_id=1, source_target_pairs={{0,2},{1,3},{2,0},{3,1},{4,6},{5,7},{6,4},{7,5},{8,10},{9,11},{10,... | collective-permute-start | bytes 12582920 | tf_op jit(solution)/shard_map/ppermute | solution.py:401
  58.8 376.5 %collective-permute-start.7 = (bf16[4,512,1024]{2,1,0:T(8,128)(2,1)}, bf16[4,512,1024]{2,1,0:T(8,128)(2,1)}, u32[]{:S(2)}, u32[]{:S(2)}) collective-permute-start(bf16[4,512,1024]{2,1,0:T(8,128)(2,1)} %pad_maximum_fusion.2), channel_id=1, source_target_pairs={{0,3},{1,2},{2,1},{3,0},{4,7},{5,6},{6,5},{7,4},{8,11},{9,10},{10,... | collective-permute-start | bytes 12582920 | tf_op jit(solution)/shard_map/ppermute | solution.py:401
  64.7 133.0 %copy-start.36 = (f32[128]{0:T(128)}, f32[128]{0:T(128)S(1)}, u32[]{:S(2)}) copy-start(f32[128]{0:T(128)S(1)} %add_rsqrt_fusion.1) | copy-start | bytes 1540
  65.3 130.7 %copy-start.31 = (f32[1,2048]{1,0:T(1,128)}, f32[1,2048]{1,0:T(1,128)S(1)}, u32[]{:S(2)}) copy-start(f32[1,2048]{1,0:T(1,128)S(1)} %get-tuple-element.194) | copy-start | bytes 24580
  218.7 23.2 %copy-start.16 = (bf16[128,2048]{0,1:T(8,128)(2,1)S(1)}, bf16[128,2048]{0,1:T(8,128)(2,1)}, u32[]{:S(2)}) copy-start(bf16[128,2048]{0,1:T(8,128)(2,1)} %get-tuple-element.176) | copy-start | bytes 1572868
  235.7 18.2 %all-to-all-start.2 = ((bf16[16,128,128]{2,1,0:T(8,128)(2,1)}), bf16[16,128,128]{2,1,0:T(8,128)(2,1)S(1)}, u32[]{:S(2)}, u32[]{:S(2)}) async-start(bf16[16,128,128]{2,1,0:T(8,128)(2,1)} %bitcast.26), calls=%async_computation.2 | async-start | bytes 1048576 | tf_op jit(solution)/shard_map/all_to_all | solution.py:1637
  258.8 362.8 %copy-start.5 = (f32[128,2048]{1,0:T(8,128)}, f32[128,2048]{1,0:T(8,128)S(1)}, u32[]{:S(2)}) copy-start(f32[128,2048]{1,0:T(8,128)S(1)} %get-tuple-element.159) | copy-start | bytes 3145732
  435.2 52.0 %copy-start.2 = (s32[16,4,256]{2,1,0:T(4,128)S(1)}, s32[16,4,256]{2,1,0:T(4,128)}, u32[]{:S(2)}) copy-start(s32[16,4,256]{2,1,0:T(4,128)} %copy-done.1) | copy-start | bytes 196612
  593.1 28.5 %copy-start.18 = (f32[64,2048]{1,0:T(8,128)S(1)}, f32[64,2048]{1,0:T(8,128)}, u32[]{:S(2)}) copy-start(f32[64,2048]{1,0:T(8,128)} %get-tuple-element.182) | copy-start | bytes 1572868
  619.7 58.0 %copy-start.28 = (bf16[128,1024]{1,0:T(8,128)(2,1)S(1)}, bf16[128,1024]{1,0:T(8,128)(2,1)}, u32[]{:S(2)}) copy-start(bf16[128,1024]{1,0:T(8,128)(2,1)} %constant_dynamic-slice_fusion.5) | copy-start | bytes 786436
  619.7 110.5 %collective-permute-start.9 = (bf16[4,512,1024]{2,1,0:T(8,128)(2,1)}, bf16[4,512,1024]{2,1,0:T(8,128)(2,1)}, u32[]{:S(2)}, u32[]{:S(2)}) collective-permute-start(bf16[4,512,1024]{2,1,0:T(8,128)(2,1)} %get-tuple-element.131), channel_id=1, source_target_pairs={{0,3},{1,2},{2,1},{3,0},{4,7},{5,6},{6,5},{7,4},{8,11},{9,10},{10,... | collective-permute-start | bytes 12582920 | tf_op jit(solution)/shard_map/ppermute | solution.py:401
  619.8 350.3 %collective-permute-start.13 = (bf16[4,512,1024]{2,1,0:T(8,128)(2,1)}, bf16[4,512,1024]{2,1,0:T(8,128)(2,1)}, u32[]{:S(2)}, u32[]{:S(2)}) collective-permute-start(bf16[4,512,1024]{2,1,0:T(8,128)(2,1)} %get-tuple-element.143), channel_id=1, source_target_pairs={{0,1},{1,0},{2,3},{3,2},{4,5},{5,4},{6,7},{7,6},{8,9},{9,8},{10,11... | collective-permute-start | bytes 12582920 | tf_op jit(solution)/shard_map/ppermute | solution.py:401
  621.0 341.2 %collective-permute-start.14 = (bf16[4,256,2048]{2,1,0:T(8,128)(2,1)}, bf16[4,256,2048]{2,1,0:T(8,128)(2,1)}, u32[]{:S(2)}, u32[]{:S(2)}) collective-permute-start(bf16[4,256,2048]{2,1,0:T(8,128)(2,1)} %get-tuple-element.149), channel_id=1, source_target_pairs={{0,1},{1,0},{2,3},{3,2},{4,5},{5,4},{6,7},{7,6},{8,9},{9,8},{10,11... | collective-permute-start | bytes 12582920 | tf_op jit(solution)/shard_map/ppermute | solution.py:397
  624.4 57.4 %copy-start.29 = (bf16[128,1024]{1,0:T(8,128)(2,1)S(1)}, bf16[128,1024]{1,0:T(8,128)(2,1)}, u32[]{:S(2)}) copy-start(bf16[128,1024]{1,0:T(8,128)(2,1)} %constant_dynamic-slice_fusion.4) | copy-start | bytes 786436
  676.6 129.3 %collective-permute-start.10 = (bf16[4,512,1024]{2,1,0:T(8,128)(2,1)}, bf16[4,512,1024]{2,1,0:T(8,128)(2,1)}, u32[]{:S(2)}, u32[]{:S(2)}) collective-permute-start(bf16[4,512,1024]{2,1,0:T(8,128)(2,1)} %get-tuple-element.134), channel_id=1, source_target_pairs={{0,2},{1,3},{2,0},{3,1},{4,6},{5,7},{6,4},{7,5},{8,10},{9,11},{10,... | collective-permute-start | bytes 12582920 | tf_op jit(solution)/shard_map/ppermute | solution.py:401
  730.1 75.8 %copy-start.32 = (f32[1,2048]{1,0:T(1,128)S(1)}, f32[1,2048]{1,0:T(1,128)}, u32[]{:S(2)}) copy-start(f32[1,2048]{1,0:T(1,128)} %copy-done.31) | copy-start | bytes 24580
  730.1 75.8 %copy-start.37 = (f32[128]{0:T(128)S(1)}, f32[128]{0:T(128)}, u32[]{:S(2)}) copy-start(f32[128]{0:T(128)} %copy-done.36) | copy-start | bytes 1540
  730.1 79.0 %copy-start.17 = (bf16[2048,64]{1,0:T(8,128)(2,1)S(1)}, bf16[2048,64]{1,0:T(8,128)(2,1)}, u32[]{:S(2)}) copy-start(bf16[2048,64]{1,0:T(8,128)(2,1)} %copy.184) | copy-start | bytes 786436
  938.0 58.2 %all-to-all-start.3 = ((bf16[4,64,2048]{2,1,0:T(8,128)(2,1)}), bf16[4,64,2048]{2,1,0:T(8,128)(2,1)S(1)}, u32[]{:S(2)}, u32[]{:S(2)}) async-start(bf16[4,64,2048]{2,1,0:T(8,128)(2,1)} %broadcast_select_fusion), calls=%async_computation.3 | async-start | bytes 2097152 | tf_op jit(solution)/shard_map/all_to_all | solution.py:423
  945.4 46.6 %collective-permute-start.11 = (bf16[64,2048]{1,0:T(8,128)(2,1)}, bf16[64,2048]{1,0:T(8,128)(2,1)}, u32[]{:S(2)}, u32[]{:S(2)}) collective-permute-start(bf16[64,2048]{1,0:T(8,128)(2,1)} %get-tuple-element.184), channel_id=1, source_target_pairs={{0,2},{2,0},{1,3},{3,1},{4,6},{6,4},{5,7},{7,5},{8,10},{10,8},{9,1... | collective-permute-start | bytes 786440 | tf_op jit(solution)/shard_map/ppermute | solution.py:393
  948.2 45.8 %collective-permute-start.12 = (f32[64,2048]{1,0:T(8,128)}, f32[64,2048]{1,0:T(8,128)}, u32[]{:S(2)}, u32[]{:S(2)}) collective-permute-start(f32[64,2048]{1,0:T(8,128)} %get-tuple-element.180), channel_id=1, source_target_pairs={{0,2},{2,0},{1,3},{3,1},{4,6},{6,4},{5,7},{7,5},{8,10},{10,8},{9,1... | collective-permute-start | bytes 1572872 | tf_op jit(solution)/shard_map/ppermute | solution.py:393
  970.1 23.8 %copy-start.15 = (f32[1,64,2048]{2,1,0:T(8,128)S(1)}, f32[1,64,2048]{2,1,0:T(8,128)}, u32[]{:S(2)}) copy-start(f32[1,64,2048]{2,1,0:T(8,128)} %get-tuple-element.179) | copy-start | bytes 1572868
  (31 other events, 258.3 us)
